TPU v7x, 256 devices: a whole 4x4x8 slice. The times are simulated.
256 devices in a mesh: dp: 8 (over x, y_lo), owner: 32 (over z, y_hi, core).
Axes of the slice: x: 4, y: 4 (y_hi: 2, y_lo: 2; y = y_hi * 2 + y_lo), z: 8, core: 2. Of those that a mesh axis runs over, the one named last changes fastest.
Arguments:
- grad_parts: bfloat16 [8, 256, 512, 512], P('dp', None, 'owner'), may hold values from -6 to 6
- owner_of: int32 [256], replicated, may hold values from 0 to 255, as said below
- refresh: int32 [32], replicated, may hold values from 0 to 255, as said below
- left_stat: float32 [256, 512, 512], P(('dp', 'owner')), may hold values from -0.05 to 0.1, as said below
- right_stat: float32 [256, 512, 512], P(('dp', 'owner')), may hold values from -0.05 to 0.1, as said below
- left_root: float32 [256, 512, 512], P(('dp', 'owner')), may hold values from -1 to 4, as said below
- right_root: float32 [256, 512, 512], P(('dp', 'owner')), may hold values from -1 to 4, as said below
Outputs:
- update: bfloat16 [256, 512, 512], P(('dp', 'owner'))
- new_left_stat: float32 [256, 512, 512], P(('dp', 'owner'))
- new_right_stat: float32 [256, 512, 512], P(('dp', 'owner'))
- new_left_root: float32 [256, 512, 512], P(('dp', 'owner'))
- new_right_root: float32 [256, 512, 512], P(('dp', 'owner'))
Inputs may be any that keep to these rules, and one draw needn't show every extreme that they name: `owner_of`: A permutation of the blocks over the device slots. `refresh`: 32 distinct blocks; no two of them are owned by the slots 2 k and 2 k + 1 for any k. `left_stat`: each block symmetric positive definite. `right_stat`: each block symmetric positive definite. `left_root`: each block symmetric positive definite. `right_root`: each block symmetric positive definite.
All inputs are finite; a program needn't handle non-finite values.
Results may differ from a plain program's by a relative error of at most 0.034.
Values may be sent and summed in bfloat16 or wider, within the bound.
No kernel may reach another device: no remote copies, remote signals or barrier semaphores. Data moves between devices by JAX's collectives and lax.ppermute only.
A program may use at most 64 MiB of HBM per device.

v0:
```python
import jax
import jax.numpy as jnp
from jax import lax
from jax.sharding import PartitionSpec as P

ITERS = 3


DECAY = 0.9
SHARE = 0.1


def inverse_root(matrix):
    highest = lax.Precision.HIGHEST
    identity = jnp.eye(matrix.shape[0], dtype=jnp.float32)
    frob_norm = jnp.sqrt(jnp.sum(matrix * matrix))
    iterate = matrix / frob_norm
    inverse = identity
    for sweep_index in range(ITERS):
        factor = (5.0 * identity - iterate) * 0.25
        if sweep_index == 0:
            inverse = factor * lax.rsqrt(jnp.sqrt(frob_norm))
        else:
            inverse = jnp.dot(inverse, factor, precision=highest)
        if sweep_index + 1 < ITERS:
            powered = jnp.dot(factor, factor, precision=highest)
            powered = jnp.dot(powered, factor, precision=highest)
            powered = jnp.dot(powered, factor, precision=highest)
            iterate = jnp.dot(powered, iterate, precision=highest)
    return inverse


def per_device(grad_parts, owner_of, refresh, left_stat, right_stat, left_root, right_root):
    n_owner = lax.axis_size("owner")
    n_data = lax.axis_size("dp")
    block_count = owner_of.shape[0]
    block_at = (
        jnp.zeros((block_count,), jnp.int32)
        .at[owner_of]
        .set(jnp.arange(block_count, dtype=jnp.int32))
    )
    my_slot = lax.axis_index("dp") * n_owner + lax.axis_index("owner")
    shard_rows = grad_parts[0]
    row_count = shard_rows.shape[1]
    width = shard_rows.shape[2]
    slot_table = block_at.reshape(n_data, n_owner).T.reshape(-1)
    outgoing = jnp.take(shard_rows, slot_table, axis=0).reshape(n_owner, n_data, row_count, width)
    arrived = lax.all_to_all(outgoing, "owner", split_axis=0, concat_axis=2, tiled=True)
    summed = lax.psum_scatter(
        arrived.astype(jnp.float32).astype(jnp.bfloat16), "dp", scatter_dimension=1, tiled=True
    ).astype(jnp.float32)
    gradient = summed[0, 0].astype(jnp.bfloat16)
    left_old = left_stat[0]
    right_old = right_stat[0]
    left_prev = left_root[0]
    right_prev = right_root[0]
    coeff = SHARE / width
    new_left = DECAY * left_old + coeff * jnp.dot(
        gradient, gradient.T, preferred_element_type=jnp.float32
    )
    new_right = DECAY * right_old + coeff * jnp.dot(
        gradient.T, gradient, preferred_element_type=jnp.float32
    )
    left_low = left_prev.astype(jnp.bfloat16)
    right_low = right_prev.astype(jnp.bfloat16)
    left_part = jnp.dot(left_low, gradient, preferred_element_type=jnp.float32).astype(jnp.bfloat16)
    update = jnp.dot(left_part, right_low, preferred_element_type=jnp.float32).astype(jnp.bfloat16)
    my_block = block_at[my_slot]
    refreshed = jnp.any(refresh == my_block)
    fresh_left, fresh_right = lax.cond(
        refreshed,
        lambda: (inverse_root(left_old), inverse_root(right_old)),
        lambda: (left_prev, right_prev),
    )
    return (update[None], new_left[None], new_right[None], fresh_left[None], fresh_right[None])


def solution(mesh):
    return jax.shard_map(
        per_device,
        mesh=mesh,
        in_specs=(
            P("dp", None, "owner", None),
            P(),
            P(),
            P(("dp", "owner"), None, None),
            P(("dp", "owner"), None, None),
            P(("dp", "owner"), None, None),
            P(("dp", "owner"), None, None),
        ),
        out_specs=(
            P(("dp", "owner"), None, None),
            P(("dp", "owner"), None, None),
            P(("dp", "owner"), None, None),
            P(("dp", "owner"), None, None),
            P(("dp", "owner"), None, None),
        ),
        check_vma=False,
    )
```

profile of v0, /device:TPU:6, one launch (start us, length us, event | category | flops | bytes accessed | tf_op | source)
XLA Modules:
  0.0 231.8 jit_solution(8399932996763596718)
XLA Ops:
  7.2 0.0 reduce-scatter.2.cloned.1.call-start
  7.2 0.7 compare_select_fusion.2
  7.9 1.4 scatter_custom_fusion
  9.3 0.1 reshape.60
  9.4 0.1 copy.14
  9.5 0.1 reshape.61
  9.6 0.1 copy.13
  9.7 4.9 %gather_fusion = bf16[256,16,512]{2,1,0:T(8,128)(2,1)} fusion(bf16[256,16,512]{2,1,0:T(8,128)(2,1)} %bitcast.74, s32[1024]{0:T(1024)S(1)} %pad_clamp_fusion), kind=kCustom, calls=%fused_computation | custom fusion | bytes 8389632 | tf_op jit(solution)/shard_map/jit(_take)/gather | solution.py:47
  14.6 2.5 %broadcast_select_fusion = bf16[32,8,16,512]{3,2,1,0:T(8,128)(2,1)S(1)} fusion(bf16[32,8,16,512]{3,2,1,0:T(8,128)(2,1)} %bitcast.71, pred[32,8]{1,0:T(8,128)(4,1)S(1)} %copy.13), kind=kLoop, calls=%fused_computation.93 | loop fusion | flops 2097152 | bytes 8388864 | tf_op jit(solution)/shard_map/jit(_take)/select_n | solution.py:47
  17.1 107.8 %all_to_all.18 = bf16[32,8,16,512]{3,2,1,0:T(8,128)(2,1)S(1)} all-to-all(bf16[32,8,16,512]{3,2,1,0:T(8,128)(2,1)S(1)} %broadcast_select_fusion), channel_id=1, replica_groups=mesh['dp'=8,'owner'=32] {'owner'}, dimensions={0} | all-to-all | bytes 8388608 | tf_op jit(solution)/shard_map/all_to_all | solution.py:48
  124.9 2.4 %copy.15 = bf16[1,8,32,16,512]{4,3,2,1,0:T(8,128)(2,1)} copy(bf16[1,8,32,16,512]{4,3,1,2,0:T(8,128)(2,1)S(1)} %bitcast.70) | data formatting | bytes 8388608 | tf_op jit(solution)/shard_map/all_to_all | solution.py:48
  127.3 0.0 copy-start.5
  127.3 0.0 copy-start.1
  127.3 0.0 copy-start.2
  127.3 0.0 copy-start.3
  127.3 0.0 reduce-scatter.2.cloned.1.call-update
  127.4 0.6 dynamic_slice.3
  127.9 0.0 copy-done.5
  128.0 1.6 compare_reduce_fusion
  130.2 0.0 copy-done.1
  130.2 0.0 copy-done.2
  130.2 0.0 copy-done.3
  130.2 2.0 conditional.1
  130.3 1.0 copy.16
  131.2 1.0 copy.17
  132.2 84.3 %reduce-scatter.2.cloned.1.call-done = bf16[1,1,512,512]{3,2,1,0:T(8,128)(2,1)} async-done(((bf16[1,8,512,512]{3,2,1,0:T(8,128)(2,1)}), bf16[1,1,512,512]{3,2,1,0:T(8,128)(2,1)}) %reduce-scatter.2.cloned.1.call-update) | async-done | bytes 524304 | tf_op jit(solution)/shard_map/reduce_scatter | solution.py:49
  216.5 0.0 copy-start
  216.5 2.8 %fusion.90 = bf16[1,512,512]{2,1,0:T(8,128)(2,1)} fusion(bf16[1,1,512,512]{3,2,1,0:T(8,128)(2,1)} %reduce-scatter.2.cloned.1.call-done, f32[1,512,512]{2,1,0:T(8,128)S(1)} %copy-done.1, f32[1,512,512]{2,1,0:T(8,128)S(1)} %copy-done.2), kind=kOutput, calls=%fused_computation.102 | convolution fusion | flops 537395200 | bytes 3145728 | tf_op jit(solution)/shard_map/dot_general | solution.py:67
  219.3 3.0 %fusion.89 = f32[1,512,512]{2,1,0:T(8,128)} fusion(bf16[1,1,512,512]{3,2,1,0:T(8,128)(2,1)} %reduce-scatter.2.cloned.1.call-done, f32[1,512,512]{2,1,0:T(8,128)} %param.12), kind=kOutput, calls=%fused_computation.99 | convolution fusion | flops 269221888 | bytes 2621440 | tf_op jit(solution)/shard_map/dot_general | solution.py:58
  222.3 0.0 copy-done
  222.3 2.7 %fusion.87 = f32[1,512,512]{2,1,0:T(8,128)} fusion(bf16[1,1,512,512]{3,2,1,0:T(8,128)(2,1)S(1)} %copy-done, f32[1,512,512]{2,1,0:T(8,128)} %param.13), kind=kOutput, calls=%fused_computation.96 | convolution fusion | flops 269221888 | bytes 2621440 | tf_op jit(solution)/shard_map/dot_general | solution.py:61
  (4 shorter events, 0.0 us)
Async XLA Ops:
  7.2 209.4 %reduce-scatter.2.cloned.1.call-start = ((), (), s32[]{:S(2)}) async-start(), calls=%async_computation.2 | async-start | bytes 4718592 | tf_op jit(solution)/shard_map/reduce_scatter | solution.py:49
  127.3 0.7 copy-start.5
  127.3 2.9 %copy-start.1 = (f32[1,512,512]{2,1,0:T(8,128)S(1)}, f32[1,512,512]{2,1,0:T(8,128)}, u32[]{:S(2)}) copy-start(f32[1,512,512]{2,1,0:T(8,128)} %param.14) | copy-start | bytes 3145732
  127.3 2.9 %copy-start.2 = (f32[1,512,512]{2,1,0:T(8,128)S(1)}, f32[1,512,512]{2,1,0:T(8,128)}, u32[]{:S(2)}) copy-start(f32[1,512,512]{2,1,0:T(8,128)} %param.15) | copy-start | bytes 3145732
  127.3 2.9 %copy-start.3 = (f32[1,512,512]{2,1,0:T(8,128)S(1)}, f32[1,512,512]{2,1,0:T(8,128)}, u32[]{:S(2)}) copy-start(f32[1,512,512]{2,1,0:T(8,128)} %param.12) | copy-start | bytes 3145732
  216.5 5.8 %copy-start = (bf16[1,1,512,512]{3,2,1,0:T(8,128)(2,1)S(1)}, bf16[1,1,512,512]{3,2,1,0:T(8,128)(2,1)}, u32[]{:S(2)}) copy-start(bf16[1,1,512,512]{3,2,1,0:T(8,128)(2,1)} %reduce-scatter.2.cloned.1.call-done) | copy-start | bytes 1572868
Sparse Core Ops, SparseCore 0:
  127.5 89.0 reduce-scatter.1
where the time goes:
time: 236 us; the launch traced here: 232 us
  blocking collectives  108 us (46%)
  waiting for transfers between devices  84.3 us (36%)
  between operations  14.8 us (6%)
  local copies, waits for them, and re-layouts  11.6 us (5%)
  matrix products  8.43 us (4%)
  other arithmetic  4.79 us (2%)
    all_to_all x1, blocking collectives, per_device(): lax.all_to_all(outgoing, 'owner', split_axis=0, concat_axis=2, tiled=True)  108 us
    reduce_scatter x1, waiting for transfers between devices, per_device(): lax.psum_scatter(arrived.astype(jnp.float32).astype(jnp.bfloat16), 'dp',...  84.3 us
    gather x1, local copies, waits for them, and re-layouts, per_device(): jnp.take(shard_rows, slot_table, axis=0)  4.93 us
  transfers between devices with their start and end apart: 1, of which 1 were waited for; matrix products, arithmetic and copies ran while one was open for 2% of the time, Pallas kernels for 0%

commit v1 on v0

v1 whole, which is shorter than its diff:
```python
import functools

import jax
import jax.numpy as jnp
import numpy as np
from jax import lax
from jax.experimental import pallas as pl
from jax.experimental.pallas import tpu as pltpu
from jax.sharding import PartitionSpec as P

DECAY = 0.9
SHARE = 0.1
AXES = ("dp", "owner")
MIB = 1 << 20

ORDERS = {0: (("a", "y", "b"), ("y", "b", "a")), 1: (("b", "a", "y"), ("y", "b", "a"))}


def split_slot(slot, n_owner):
    data, owner = divmod(slot, n_owner)
    return data // 2, data % 2, owner


def join_slot(x, y_lo, owner, n_owner):
    return (x * 2 + y_lo) * n_owner + owner


def flip(slot, dim, n_owner):
    x, y_lo, owner = split_slot(slot, n_owner)
    if dim == "a":
        x ^= 1
    elif dim == "b":
        x ^= 3
    else:
        y_lo ^= 1
    return join_slot(x, y_lo, owner, n_owner)


def exchange(n_slots, n_owner, part, step):
    return [(s, flip(s, ORDERS[s % 2][part][step], n_owner)) for s in range(n_slots)]


def slot_rows(n_slots, n_owner, cuts):
    rows = np.zeros((n_slots, 2, n_slots // 2), np.int32)
    for s in range(n_slots):
        x, y_lo, _ = split_slot(s, n_owner)
        for kind, first in ((0, 1), (1, 0)):
            out = []
            for part in range(2):
                one, two, three = ORDERS[s % 2][part]
                for second in (0, 1):
                    for third in (0, 1):
                        for owner in range(cuts[part], cuts[part + 1]):
                            t = join_slot(x, y_lo, owner, n_owner)
                            for dim, bit in ((one, first), (two, second), (three, third)):
                                t = flip(t, dim, n_owner) if bit else t
                            out.append(t)
            rows[s, kind] = out
    return rows


def pick_kernel(owner_ref, slots_ref, shard_ref, first_ref, second_ref, held, block_at, sem):
    copy = pltpu.make_async_copy(shard_ref, held, sem)
    copy.start()

    @pl.loop(0, owner_ref.shape[0], unroll=8)
    def _(b):
        block_at[owner_ref[b]] = b

    copy.wait()
    offset = 0
    for out in (first_ref, second_ref):

        @pl.loop(0, out.shape[0], unroll=4)
        def _(i, out=out, offset=offset):
            out[i] = held[block_at[slots_ref[offset + i]]]

        offset += out.shape[0]


def pick(owner_of, slots, shard_rows, counts):
    _, rows, width = shard_rows.shape
    vmem = pl.BlockSpec(memory_space=pltpu.VMEM)
    smem = pl.BlockSpec(memory_space=pltpu.SMEM)
    return pl.pallas_call(
        pick_kernel,
        out_shape=[jax.ShapeDtypeStruct((n, rows, width), shard_rows.dtype) for n in counts],
        in_specs=[smem, smem, pl.BlockSpec(memory_space=pl.ANY)],
        out_specs=[vmem] * 2,
        scratch_shapes=[
            pltpu.VMEM(shard_rows.shape, shard_rows.dtype),
            pltpu.SMEM(owner_of.shape, jnp.int32),
            pltpu.SemaphoreType.DMA,
        ],
        compiler_params=pltpu.CompilerParams(vmem_limit_bytes=16 * MIB),
        cost_estimate=pl.CostEstimate(flops=0, bytes_accessed=12 * MIB, transcendentals=0),
    )(owner_of, slots, shard_rows)


def times(a, b):
    return jnp.dot(
        a.astype(jnp.bfloat16), b.astype(jnp.bfloat16), preferred_element_type=jnp.float32
    )


def next_iterate(m):
    d = (times(m, m) - 10.0 * m) * (1.0 / 16.0)
    e = times(d, d) + 3.125 * d
    return (625.0 / 256.0) * m + times(e, m)


def root_of(stat):
    c = jnp.sqrt(jnp.sum(stat * stat))
    m0 = stat / c
    m1 = next_iterate(m0)
    m2 = next_iterate(m1)
    t = times(m0, m1)
    pair = m0 + m1
    total = times(5.0 * pair - t, m2) + 5.0 * t - 25.0 * (pair + m2)
    n = stat.shape[0]
    on_diagonal = lax.broadcasted_iota(jnp.int32, (n, n), 0) == lax.broadcasted_iota(
        jnp.int32, (n, n), 1
    )
    total = total + jnp.where(on_diagonal, 125.0, 0.0)
    return total * (lax.rsqrt(jnp.sqrt(c)) * (1.0 / 64.0))


def roots_kernel(owner_ref, refresh_ref, slot_ref, stat_ref, root_ref, out_ref):
    slot = slot_ref[0]

    def look(i, found):
        return found | jnp.where(owner_ref[refresh_ref[i]] == slot, 1, 0)

    fresh = lax.fori_loop(0, refresh_ref.shape[0], look, jnp.int32(0))

    @pl.when(fresh == 1)
    def _():
        out_ref[...] = root_of(stat_ref[...])

    @pl.when(fresh == 0)
    def _():
        out_ref[...] = root_ref[...]


def roots(owner_of, refresh, slot, stat, root):
    vmem = pl.BlockSpec(memory_space=pltpu.VMEM)
    smem = pl.BlockSpec(memory_space=pltpu.SMEM)
    return pl.pallas_call(
        roots_kernel,
        out_shape=jax.ShapeDtypeStruct(stat.shape, stat.dtype),
        in_specs=[smem, smem, smem, vmem, vmem],
        out_specs=vmem,
        compiler_params=pltpu.CompilerParams(vmem_limit_bytes=32 * MIB),
        cost_estimate=pl.CostEstimate(flops=8 * 2 * 512**3, bytes_accessed=3 * MIB, transcendentals=0),
    )(owner_of, refresh, slot, stat, root)


def finish_kernel(grad_ref, ls_ref, rs_ref, lr_ref, rr_ref, up_ref, nl_ref, nr_ref):
    grad = grad_ref[...]
    coeff = SHARE / grad.shape[1]
    f32 = jnp.float32
    left_part = jnp.dot(lr_ref[...].astype(jnp.bfloat16), grad, preferred_element_type=f32)
    up_ref[...] = jnp.dot(
        left_part.astype(jnp.bfloat16),
        rr_ref[...].astype(jnp.bfloat16),
        preferred_element_type=f32,
    ).astype(jnp.bfloat16)
    gram = lax.dot_general(grad, grad, (((1,), (1,)), ((), ())), preferred_element_type=f32)
    nl_ref[...] = DECAY * ls_ref[...] + coeff * gram
    gram = lax.dot_general(grad, grad, (((0,), (0,)), ((), ())), preferred_element_type=f32)
    nr_ref[...] = DECAY * rs_ref[...] + coeff * gram


def finish(grad, left_stat, right_stat, left_root, right_root):
    vmem = pl.BlockSpec(memory_space=pltpu.VMEM)
    return pl.pallas_call(
        finish_kernel,
        out_shape=[
            jax.ShapeDtypeStruct(grad.shape, jnp.bfloat16),
            jax.ShapeDtypeStruct(left_stat.shape, jnp.float32),
            jax.ShapeDtypeStruct(right_stat.shape, jnp.float32),
        ],
        in_specs=[vmem] * 5,
        out_specs=[vmem] * 3,
        compiler_params=pltpu.CompilerParams(vmem_limit_bytes=32 * MIB),
        cost_estimate=pl.CostEstimate(flops=4 * 2 * 512**3, bytes_accessed=7 * MIB, transcendentals=0),
    )(grad, left_stat, right_stat, left_root, right_root)


def plus(a, b):
    return (a.astype(jnp.float32) + b.astype(jnp.float32)).astype(jnp.bfloat16)


def per_device(grad_parts, owner_of, refresh, left_stat, right_stat, left_root, right_root):
    n_owner = lax.axis_size("owner")
    n_slots = lax.axis_size("dp") * n_owner
    my_slot = lax.axis_index("dp") * n_owner + lax.axis_index("owner")
    shard_rows = grad_parts[0]
    cuts = (0, (2 * n_owner) // 3, n_owner)
    table = slot_rows(n_slots, n_owner, cuts)
    mine = lax.dynamic_index_in_dim(jnp.asarray(table), my_slot, 0, keepdims=False)
    counts = [4 * (cuts[1] - cuts[0]), 4 * (cuts[2] - cuts[1])]
    sent = pick(owner_of, mine[0], shard_rows, counts)
    kept = pick(owner_of, mine[1], shard_rows, counts)
    summed = []
    for step in range(3):
        arrived = [
            lax.ppermute(s, AXES, exchange(n_slots, n_owner, part, step))
            for part, s in enumerate(sent)
        ]
        if step == 2:
            summed = [plus(a, k) for a, k in zip(arrived, kept)]
        else:
            half = [a.shape[0] // 2 for a in arrived]
            sent = [plus(a[h:], k[h:]) for a, k, h in zip(arrived, kept, half)]
            kept = [plus(a[:h], k[:h]) for a, k, h in zip(arrived, kept, half)]
    outgoing = jnp.concatenate(summed, axis=0)
    grad = lax.all_to_all(outgoing, "owner", split_axis=0, concat_axis=0, tiled=True)
    grad = grad.reshape(left_stat.shape[1], -1)
    slot = my_slot.reshape(1)
    new_left_root = roots(owner_of, refresh, slot, left_stat[0], left_root[0])
    new_right_root = roots(owner_of, refresh, slot, right_stat[0], right_root[0])
    update, new_left, new_right = finish(
        grad, left_stat[0], right_stat[0], left_root[0], right_root[0]
    )
    return (
        update[None],
        new_left[None],
        new_right[None],
        new_left_root[None],
        new_right_root[None],
    )


def solution(mesh):
    owned = P(AXES, None, None)
    return jax.shard_map(
        per_device,
        mesh=mesh,
        in_specs=(P("dp", None, "owner", None), P(), P(), owned, owned, owned, owned),
        out_specs=(owned,) * 5,
        check_vma=False,
    )
```

time: 236 us -> 83.2 us (0.35); the launches traced: 232 us -> 81.6 us
  blocking collectives: 108 us -> 0 us
  waiting for transfers between devices: 84.3 us -> 37.5 us
  starting transfers between devices: 0.04 us -> 18.2 us
  Pallas kernels: 0 us -> 15.8 us
  between operations: 14.8 us -> 0.76 us
  matrix products: 8.43 us -> 0 us
  local copies, waits for them, and re-layouts: 11.6 us -> 7.26 us
  other arithmetic: 4.79 us -> 2.11 us
    all_to_all x1 -> x0, blocking collectives: 108 us -> none  [per_device(): lax.all_to_all(outgoing, 'owner', split_axis=0, concat_axis=2, tiled=True)]
    reduce_scatter x1 -> x0, waiting for transfers between devices: 84.3 us -> none  [per_device(): lax.psum_scatter(arrived.astype(jnp.float32).astype(jnp.bfloat16), 'dp',...]
    ppermute x0 -> x6, waiting for transfers between devices: none -> 30.7 us  [per_device(): lax.ppermute(s, AXES, exchange(n_slots, n_owner, part, step))]
    pallas_call x0 -> x5, Pallas kernels: none -> 15.8 us  [the longest x2 9.99 us: roots(): pl.pallas_call(roots_kernel, out_shape=jax.ShapeDtypeStruct(stat.shape, s...]
    all_to_all x0 -> x1, starting transfers between devices: none -> 11.5 us  [per_device(): lax.all_to_all(outgoing, 'owner', split_axis=0, concat_axis=0, tiled=True)]
    dot_general x3 -> x0, matrix products: 8.43 us -> none  [the longest x1 2.99 us: per_device(): jnp.dot(gradient, gradient.T, preferred_element_type=jnp.float32)]
    all_to_all x0 -> x1, waiting for transfers between devices: none -> 6.77 us  [per_device(): lax.all_to_all(outgoing, 'owner', split_axis=0, concat_axis=0, tiled=True)]
    ppermute x0 -> x6, starting transfers between devices: none -> 6.72 us  [per_device(): lax.ppermute(s, AXES, exchange(n_slots, n_owner, part, step))]
  transfers between devices with their start and end apart: 1 -> 7, of which waited for: 1 -> 5; matrix products, arithmetic and copies ran while one was open for 2% -> 1% of each run, Pallas kernels for 0% -> 14%
where the time goes in v1:
time: 83.2 us; the launch traced here: 81.6 us
  waiting for transfers between devices  37.5 us (45%)
  starting transfers between devices  18.2 us (22%)
  Pallas kernels  15.8 us (19%)
  local copies, waits for them, and re-layouts  7.26 us (9%)
  other arithmetic  2.11 us (3%)
    ppermute x6, waiting for transfers between devices, per_device(): lax.ppermute(s, AXES, exchange(n_slots, n_owner, part, step))  30.7 us
    all_to_all x1, starting transfers between devices, per_device(): lax.all_to_all(outgoing, 'owner', split_axis=0, concat_axis=0, tiled=True)  11.5 us
    pallas_call x2, Pallas kernels, roots(): pl.pallas_call(roots_kernel, out_shape=jax.ShapeDtypeStruct(stat.shape, s...  9.99 us
    all_to_all x1, waiting for transfers between devices, per_device(): lax.all_to_all(outgoing, 'owner', split_axis=0, concat_axis=0, tiled=True)  6.77 us
    ppermute x6, starting transfers between devices, per_device(): lax.ppermute(s, AXES, exchange(n_slots, n_owner, part, step))  6.72 us
    unnamed x22, local copies, waits for them, and re-layouts  6.56 us
    pallas_call x2, Pallas kernels, pick(): pl.pallas_call(pick_kernel, out_shape=[jax.ShapeDtypeStruct((n, rows, wid...  3.31 us
    pallas_call x1, Pallas kernels, finish(): pl.pallas_call(finish_kernel, out_shape=[jax.ShapeDtypeStruct(grad.shape,...  2.52 us
  transfers between devices with their start and end apart: 7, of which 5 were waited for; matrix products, arithmetic and copies ran while one was open for 1% of the time, Pallas kernels for 14%

profile of v1, /device:TPU:6, one launch (start us, length us, event | category | flops | bytes accessed | tf_op | source)
XLA Modules:
  0.0 81.6 jit_solution(15858560687325772533)
XLA Ops:
  0.6 0.7 constant_dynamic-slice_fusion
  1.3 2.2 %copy-done = bf16[1,256,16,512]{3,2,1,0:T(8,128)(2,1)S(1)} copy-done((bf16[1,256,16,512]{3,2,1,0:T(8,128)(2,1)S(1)}, bf16[1,256,16,512]{3,2,1,0:T(8,128)(2,1)}, u32[]{:S(2)}) %copy-start) | copy-done | bytes 4194328
  3.5 0.7 copy-done.8
  4.2 1.7 %shard_map.119 = (bf16[84,16,512]{2,1,0:T(8,128)(2,1)S(1)}, bf16[44,16,512]{2,1,0:T(8,128)(2,1)S(1)}) custom-call(s32[256]{0:T(256)S(1)} %copy-done.8, s32[128]{0:T(128)S(1)} %get-tuple-element.24.slots_ref, bf16[256,16,512]{2,1,0:T(8,128)(2,1)S(1)} %bitcast.16), custom_call_target="tpu_custom_call" | custom-call | bytes 12582912 | tf_op jit(solution)/shard_map/pallas_call | solution.py:85
  5.9 0.9 %collective-permute-start = (bf16[84,16,512]{2,1,0:T(8,128)(2,1)S(1)}, bf16[84,16,512]{2,1,0:T(8,128)(2,1)S(1)}, u32[]{:S(2)}, u32[]{:S(2)}) collective-permute-start(bf16[84,16,512]{2,1,0:T(8,128)(2,1)S(1)} %get-tuple-element.12), channel_id=1, source_target_pairs={{0,64},{1,193},{2,66},{3,195},{4,68},{5,197},{6,70},{7,199},{8,72}... | collective-permute-start | bytes 4128776 | tf_op jit(solution)/shard_map/ppermute | solution.py:208
  6.8 1.6 %collective-permute-start.3 = (bf16[44,16,512]{2,1,0:T(8,128)(2,1)S(1)}, bf16[44,16,512]{2,1,0:T(8,128)(2,1)S(1)}, u32[]{:S(2)}, u32[]{:S(2)}) collective-permute-start(bf16[44,16,512]{2,1,0:T(8,128)(2,1)S(1)} %get-tuple-element.14), channel_id=1, source_target_pairs={{0,32},{1,33},{2,34},{3,35},{4,36},{5,37},{6,38},{7,39},{8,40},{9,... | collective-permute-start | bytes 2162696 | tf_op jit(solution)/shard_map/ppermute | solution.py:208
  8.4 1.7 %shard_map.120 = (bf16[84,16,512]{2,1,0:T(8,128)(2,1)S(1)}, bf16[44,16,512]{2,1,0:T(8,128)(2,1)S(1)}) custom-call(s32[256]{0:T(256)S(1)} %copy-done.8, s32[128]{0:T(128)S(1)} %get-tuple-element.23.slots_ref, bf16[256,16,512]{2,1,0:T(8,128)(2,1)S(1)} %bitcast.17), custom_call_target="tpu_custom_call" | custom-call | bytes 12582912 | tf_op jit(solution)/shard_map/pallas_call | solution.py:85
  10.0 14.2 %collective-permute-done = bf16[84,16,512]{2,1,0:T(8,128)(2,1)S(1)} collective-permute-done((bf16[84,16,512]{2,1,0:T(8,128)(2,1)S(1)}, bf16[84,16,512]{2,1,0:T(8,128)(2,1)S(1)}, u32[]{:S(2)}, u32[]{:S(2)}) %collective-permute-start) | collective-permute-done | bytes 1376288 | tf_op jit(solution)/shard_map/ppermute | solution.py:208
  24.3 0.6 add_convert_fusion.1
  24.8 1.7 %collective-permute-start.1 = (bf16[42,16,512]{2,1,0:T(8,128)(2,1)S(1)}, bf16[42,16,512]{2,1,0:T(8,128)(2,1)S(1)}, u32[]{:S(2)}, u32[]{:S(2)}) collective-permute-start(bf16[42,16,512]{2,1,0:T(8,128)(2,1)S(1)} %get-tuple-element.19), channel_id=1, source_target_pairs={{0,32},{1,65},{2,34},{3,67},{4,36},{5,69},{6,38},{7,71},{8,40},{9,... | collective-permute-start | bytes 2064392 | tf_op jit(solution)/shard_map/ppermute | solution.py:208
  26.5 0.3 add_convert_fusion.3
  26.8 0.7 collective-permute-start.4
  27.5 9.2 %collective-permute-done.4 = bf16[22,16,512]{2,1,0:T(8,128)(2,1)S(1)} collective-permute-done((bf16[22,16,512]{2,1,0:T(8,128)(2,1)S(1)}, bf16[22,16,512]{2,1,0:T(8,128)(2,1)S(1)}, u32[]{:S(2)}, u32[]{:S(2)}) %collective-permute-start.4) | collective-permute-done | bytes 360480 | tf_op jit(solution)/shard_map/ppermute | solution.py:208
  36.8 0.6 collective-permute-start.5
  37.4 0.1 add_convert_fusion.6
  37.5 1.2 %collective-permute-start.2 = (bf16[21,16,512]{2,1,0:T(8,128)(2,1)S(1)}, bf16[21,16,512]{2,1,0:T(8,128)(2,1)S(1)}, u32[]{:S(2)}, u32[]{:S(2)}) collective-permute-start(bf16[21,16,512]{2,1,0:T(8,128)(2,1)S(1)} %add_convert_fusion.6), channel_id=1, source_target_pairs={{0,192},{1,33},{2,194},{3,35},{4,196},{5,37},{6,198},{7,39},{8,200... | collective-permute-start | bytes 1032200 | tf_op jit(solution)/shard_map/ppermute | solution.py:208
  38.7 3.6 %collective-permute-done.5 = bf16[11,16,512]{2,1,0:T(8,128)(2,1)S(1)} collective-permute-done((bf16[11,16,512]{2,1,0:T(8,128)(2,1)S(1)}, bf16[11,16,512]{2,1,0:T(8,128)(2,1)S(1)}, u32[]{:S(2)}, u32[]{:S(2)}) %collective-permute-start.5) | collective-permute-done | bytes 180256 | tf_op jit(solution)/shard_map/ppermute | solution.py:208
  42.4 0.1 add_convert_fusion.7
  42.5 3.6 %collective-permute-done.2 = bf16[21,16,512]{2,1,0:T(8,128)(2,1)S(1)} collective-permute-done((bf16[21,16,512]{2,1,0:T(8,128)(2,1)S(1)}, bf16[21,16,512]{2,1,0:T(8,128)(2,1)S(1)}, u32[]{:S(2)}, u32[]{:S(2)}) %collective-permute-start.2) | collective-permute-done | bytes 344096 | tf_op jit(solution)/shard_map/ppermute | solution.py:208
  46.1 0.2 add_convert_fusion.4
  46.2 0.0 copy-start.2
  46.3 0.0 copy-start.10
  46.3 0.8 %pad_maximum_fusion = bf16[32,16,512]{2,1,0:T(8,128)(2,1)} fusion(bf16[11,16,512]{2,1,0:T(8,128)(2,1)S(1)} %add_convert_fusion.7, bf16[21,16,512]{2,1,0:T(8,128)(2,1)S(1)} %add_convert_fusion.4), kind=kLoop, calls=%fused_computation.7 | loop fusion | flops 262144 | bytes 1048576 | tf_op jit(solution)/shard_map/concatenate | solution.py:217
  47.1 11.5 %all-to-all-start = ((bf16[32,16,512]{2,1,0:T(8,128)(2,1)}), bf16[32,16,512]{2,1,0:T(8,128)(2,1)S(1)}, u32[]{:S(2)}, u32[]{:S(2)}) async-start(bf16[32,16,512]{2,1,0:T(8,128)(2,1)} %pad_maximum_fusion), calls=%async_computation | async-start | bytes 1048576 | tf_op jit(solution)/shard_map/all_to_all | solution.py:218
  58.7 0.0 copy-start.4
  58.7 1.2 %copy-done.4 = f32[1,512,512]{2,1,0:T(8,128)S(1)} copy-done((f32[1,512,512]{2,1,0:T(8,128)S(1)}, f32[1,512,512]{2,1,0:T(8,128)}, u32[]{:S(2)}) %copy-start.4) | copy-done | bytes 1048600
  59.9 5.0 %shard_map.122 = f32[512,512]{1,0:T(8,128)} custom-call(s32[256]{0:T(256)S(1)} %copy-done.9, s32[32]{0:T(128)S(1)} %copy-done.10, s32[1]{0:T(128)} %bitcast.11.slot_ref, f32[512,512]{1,0:T(8,128)S(1)} %bitcast.19, f32[512,512]{1,0:T(8,128)S(1)} %bitcast.23), custom_call_target="tpu_custom_call" | custom-call | flops 2147483648 | bytes 3145728 | tf_op jit(solution)/shard_map/pallas_call | solution.py:148
  64.9 5.0 %shard_map.123 = f32[512,512]{1,0:T(8,128)} custom-call(s32[256]{0:T(256)S(1)} %copy-done.9, s32[32]{0:T(128)S(1)} %copy-done.10, s32[1]{0:T(128)} %bitcast.11.slot_ref, f32[512,512]{1,0:T(8,128)S(1)} %bitcast.21, f32[512,512]{1,0:T(8,128)S(1)} %bitcast.25), custom_call_target="tpu_custom_call" | custom-call | flops 2147483648 | bytes 3145728 | tf_op jit(solution)/shard_map/pallas_call | solution.py:148
  69.9 6.8 %all-to-all-done = bf16[32,16,512]{2,1,0:T(8,128)(2,1)S(1)} async-done(((bf16[32,16,512]{2,1,0:T(8,128)(2,1)}), bf16[32,16,512]{2,1,0:T(8,128)(2,1)S(1)}, u32[]{:S(2)}, u32[]{:S(2)}) %all-to-all-start) | async-done | bytes 524320 | tf_op jit(solution)/shard_map/all_to_all | solution.py:218
  76.7 1.2 %copy-done.5 = f32[1,512,512]{2,1,0:T(8,128)S(1)} copy-done((f32[1,512,512]{2,1,0:T(8,128)S(1)}, f32[1,512,512]{2,1,0:T(8,128)}, u32[]{:S(2)}) %copy-start.5) | copy-done | bytes 1048600
  77.9 1.2 %copy-done.7 = f32[1,512,512]{2,1,0:T(8,128)S(1)} copy-done((f32[1,512,512]{2,1,0:T(8,128)S(1)}, f32[1,512,512]{2,1,0:T(8,128)}, u32[]{:S(2)}) %copy-start.7) | copy-done | bytes 1048600
  79.1 2.5 %shard_map.121 = (bf16[512,512]{1,0:T(8,128)(2,1)}, f32[512,512]{1,0:T(8,128)}, f32[512,512]{1,0:T(8,128)}) custom-call(bf16[512,512]{1,0:T(8,128)(2,1)S(1)} %bitcast.18, f32[512,512]{1,0:T(8,128)S(1)} %bitcast.20, f32[512,512]{1,0:T(8,128)S(1)} %bitcast.22, f32[512,512]{1,0:T(8,128)S(1)} %bitcast.24, f32[512,512]{1,0:T(8,128)S(1)} %bitcast.26), custom_call_target="tpu_custom_call" | custom-call | flops 1073741824 | bytes 7340032 | tf_op jit(solution)/shard_map/pallas_call | solution.py:176
  (18 shorter events, 0.1 us)
Async XLA Ops:
  1.3 2.2 %copy-start = (bf16[1,256,16,512]{3,2,1,0:T(8,128)(2,1)S(1)}, bf16[1,256,16,512]{3,2,1,0:T(8,128)(2,1)}, u32[]{:S(2)}) copy-start(bf16[1,256,16,512]{3,2,1,0:T(8,128)(2,1)} %param.8) | copy-start | bytes 12582916
  3.5 0.7 copy-start.8
  4.2 4.2 %copy-start.1 = (bf16[1,256,16,512]{3,2,1,0:T(8,128)(2,1)S(1)}, bf16[1,256,16,512]{3,2,1,0:T(8,128)(2,1)}, u32[]{:S(2)}) copy-start(bf16[1,256,16,512]{3,2,1,0:T(8,128)(2,1)} %param.8) | copy-start | bytes 12582916
  5.9 18.4 %collective-permute-start = (bf16[84,16,512]{2,1,0:T(8,128)(2,1)S(1)}, bf16[84,16,512]{2,1,0:T(8,128)(2,1)S(1)}, u32[]{:S(2)}, u32[]{:S(2)}) collective-permute-start(bf16[84,16,512]{2,1,0:T(8,128)(2,1)S(1)} %get-tuple-element.12), channel_id=1, source_target_pairs={{0,64},{1,193},{2,66},{3,195},{4,68},{5,197},{6,70},{7,199},{8,72}... | collective-permute-start | bytes 4128776 | tf_op jit(solution)/shard_map/ppermute | solution.py:208
  6.8 19.7 %collective-permute-start.3 = (bf16[44,16,512]{2,1,0:T(8,128)(2,1)S(1)}, bf16[44,16,512]{2,1,0:T(8,128)(2,1)S(1)}, u32[]{:S(2)}, u32[]{:S(2)}) collective-permute-start(bf16[44,16,512]{2,1,0:T(8,128)(2,1)S(1)} %get-tuple-element.14), channel_id=1, source_target_pairs={{0,32},{1,33},{2,34},{3,35},{4,36},{5,37},{6,38},{7,39},{8,40},{9,... | collective-permute-start | bytes 2162696 | tf_op jit(solution)/shard_map/ppermute | solution.py:208
  24.8 12.6 %collective-permute-start.1 = (bf16[42,16,512]{2,1,0:T(8,128)(2,1)S(1)}, bf16[42,16,512]{2,1,0:T(8,128)(2,1)S(1)}, u32[]{:S(2)}, u32[]{:S(2)}) collective-permute-start(bf16[42,16,512]{2,1,0:T(8,128)(2,1)S(1)} %get-tuple-element.19), channel_id=1, source_target_pairs={{0,32},{1,65},{2,34},{3,67},{4,36},{5,69},{6,38},{7,71},{8,40},{9,... | collective-permute-start | bytes 2064392 | tf_op jit(solution)/shard_map/ppermute | solution.py:208
  26.8 10.0 %collective-permute-start.4 = (bf16[22,16,512]{2,1,0:T(8,128)(2,1)S(1)}, bf16[22,16,512]{2,1,0:T(8,128)(2,1)S(1)}, u32[]{:S(2)}, u32[]{:S(2)}) collective-permute-start(bf16[22,16,512]{2,1,0:T(8,128)(2,1)S(1)} %get-tuple-element.21), channel_id=1, source_target_pairs={{0,192},{1,193},{2,194},{3,195},{4,196},{5,197},{6,198},{7,199},{8... | collective-permute-start | bytes 1081352 | tf_op jit(solution)/shard_map/ppermute | solution.py:208
  36.8 5.6 %collective-permute-start.5 = (bf16[11,16,512]{2,1,0:T(8,128)(2,1)S(1)}, bf16[11,16,512]{2,1,0:T(8,128)(2,1)S(1)}, u32[]{:S(2)}, u32[]{:S(2)}) collective-permute-start(bf16[11,16,512]{2,1,0:T(8,128)(2,1)S(1)} %add_convert_fusion.9), channel_id=1, source_target_pairs={{0,64},{1,65},{2,66},{3,67},{4,68},{5,69},{6,70},{7,71},{8,72},{9,... | collective-permute-start | bytes 540680 | tf_op jit(solution)/shard_map/ppermute | solution.py:208
  37.5 8.5 %collective-permute-start.2 = (bf16[21,16,512]{2,1,0:T(8,128)(2,1)S(1)}, bf16[21,16,512]{2,1,0:T(8,128)(2,1)S(1)}, u32[]{:S(2)}, u32[]{:S(2)}) collective-permute-start(bf16[21,16,512]{2,1,0:T(8,128)(2,1)S(1)} %add_convert_fusion.6), channel_id=1, source_target_pairs={{0,192},{1,33},{2,194},{3,35},{4,196},{5,37},{6,198},{7,39},{8,200... | collective-permute-start | bytes 1032200 | tf_op jit(solution)/shard_map/ppermute | solution.py:208
  46.2 12.4 %copy-start.2 = (f32[1,512,512]{2,1,0:T(8,128)S(1)}, f32[1,512,512]{2,1,0:T(8,128)}, u32[]{:S(2)}) copy-start(f32[1,512,512]{2,1,0:T(8,128)} %param.11) | copy-start | bytes 3145732
  46.3 12.4 %copy-start.9 = (s32[256]{0:T(256)S(1)}, s32[256]{0:T(256)}, u32[]{:S(2)}) copy-start(s32[256]{0:T(256)} %owner_ref.7) | copy-start | bytes 3076
  46.3 12.4 %copy-start.10 = (s32[32]{0:T(128)S(1)}, s32[32]{0:T(128)}, u32[]{:S(2)}) copy-start(s32[32]{0:T(128)} %refresh_ref.3) | copy-start | bytes 388
  47.1 29.5 %all-to-all-start = ((bf16[32,16,512]{2,1,0:T(8,128)(2,1)}), bf16[32,16,512]{2,1,0:T(8,128)(2,1)S(1)}, u32[]{:S(2)}, u32[]{:S(2)}) async-start(bf16[32,16,512]{2,1,0:T(8,128)(2,1)} %pad_maximum_fusion), calls=%async_computation | async-start | bytes 1048576 | tf_op jit(solution)/shard_map/all_to_all | solution.py:218
  58.7 1.2 %copy-start.4 = (f32[1,512,512]{2,1,0:T(8,128)S(1)}, f32[1,512,512]{2,1,0:T(8,128)}, u32[]{:S(2)}) copy-start(f32[1,512,512]{2,1,0:T(8,128)} %param.13) | copy-start | bytes 3145732
  59.9 5.0 %copy-start.3 = (f32[1,512,512]{2,1,0:T(8,128)S(1)}, f32[1,512,512]{2,1,0:T(8,128)}, u32[]{:S(2)}) copy-start(f32[1,512,512]{2,1,0:T(8,128)} %param.12) | copy-start | bytes 3145732
  59.9 5.0 %copy-start.6 = (f32[1,512,512]{2,1,0:T(8,128)S(1)}, f32[1,512,512]{2,1,0:T(8,128)}, u32[]{:S(2)}) copy-start(f32[1,512,512]{2,1,0:T(8,128)} %param.14) | copy-start | bytes 3145732
  76.7 1.2 %copy-start.5 = (f32[1,512,512]{2,1,0:T(8,128)S(1)}, f32[1,512,512]{2,1,0:T(8,128)}, u32[]{:S(2)}) copy-start(f32[1,512,512]{2,1,0:T(8,128)} %param.13) | copy-start | bytes 3145732
  77.9 1.2 %copy-start.7 = (f32[1,512,512]{2,1,0:T(8,128)S(1)}, f32[1,512,512]{2,1,0:T(8,128)}, u32[]{:S(2)}) copy-start(f32[1,512,512]{2,1,0:T(8,128)} %param.14) | copy-start | bytes 3145732

commit v2 on v1

v2 whole, which is shorter than its diff:
```python
import functools

import jax
import jax.numpy as jnp
import numpy as np
from jax import lax
from jax.experimental import pallas as pl
from jax.experimental.pallas import tpu as pltpu
from jax.sharding import PartitionSpec as P

DECAY = 0.9
SHARE = 0.1
AXES = ("dp", "owner")
MIB = 1 << 20

QUAD = ((0, 0), (0, 1), (1, 0), (1, 1))
WIDE = {0: ("a", "y", "b"), 1: ("b", "a", "y")}
SLIM = {0: ("y", "b", "a"), 1: ("y", "b", "a")}
STREAMS = {
    "far": ((3, 5), WIDE),
    "farthest": ((4,), SLIM),
    "middle": ((2, 6), WIDE),
    "near": ((1, 7), WIDE),
    "here": ((0,), SLIM),
}


def place(slot, n_owner):
    data, owner = divmod(slot, n_owner)
    return data // 2, 2 * ((owner // 2) % 2) + data % 2, owner // 4, owner % 2


def slot_at(x, y, z, core, n_owner):
    return (2 * x + y % 2) * n_owner + 4 * (z % (n_owner // 4)) + 2 * (y // 2) + core


def moved(slot, n_owner, dims="", rz=0, yb=0, rc=0):
    x, y, z, core = place(slot, n_owner)
    x ^= ("a" in dims) * 1 ^ ("b" in dims) * 3
    y ^= ("y" in dims) * 1 ^ yb * 3
    return slot_at(x, y, z + rz, core ^ rc, n_owner)


def route(n_slots, n_owner, **how):
    return [(s, moved(s, n_owner, **how)) for s in range(n_slots)]


def route_step(n_slots, n_owner, orders, step):
    return [
        (s, moved(s, n_owner, dims=orders[place(s, n_owner)[3]][step])) for s in range(n_slots)
    ]


def owners_of_pieces(slot, n_owner, rzs, orders, first):
    one, two, three = orders[place(slot, n_owner)[3]]
    out = []
    for second in (0, 1):
        for third in (0, 1):
            dims = one * first + two * second + three * third
            for rz in rzs:
                for yb, rc in QUAD:
                    out.append(moved(slot, n_owner, dims=dims, rz=rz, yb=yb, rc=rc))
    return out


def build_table(n_slots, n_owner):
    spans, rows = {}, []
    for s in range(n_slots):
        row = []
        for name, (rzs, orders) in STREAMS.items():
            groups = [((name, rz), (rz,)) for rz in rzs] if name == "near" else [(name, rzs)]
            for key, group in groups:
                for first in (1, 0):
                    pieces = owners_of_pieces(s, n_owner, group, orders, first)
                    spans[key, first] = (len(row), len(pieces))
                    row += pieces
        rows.append(row)
    return spans, np.asarray(rows, np.int32)


def index_kernel(owner_ref, slots_ref, out_ref, block_at):
    @pl.loop(0, owner_ref.shape[0], unroll=8)
    def _(b):
        block_at[owner_ref[b]] = b

    @pl.loop(0, slots_ref.shape[0], unroll=8)
    def _(i):
        out_ref[i] = block_at[slots_ref[i]]


def index_pieces(owner_of, slots):
    smem = pl.BlockSpec(memory_space=pltpu.SMEM)
    return pl.pallas_call(
        index_kernel,
        out_shape=jax.ShapeDtypeStruct(slots.shape, jnp.int32),
        in_specs=[smem, smem],
        out_specs=smem,
        scratch_shapes=[pltpu.SMEM(owner_of.shape, jnp.int32)],
    )(owner_of, slots)


def pick_kernel(spans, n_after, index_ref, shard_ref, *refs):
    for out, pieces in zip(refs[n_after:], spans):
        offset = 0
        for start, count in pieces:

            @pl.loop(0, count, unroll=4)
            def _(i, out=out, offset=offset, start=start):
                out[offset + i] = shard_ref[index_ref[start + i]]

            offset += count


def pick(index, shard_rows, spans, after=()):
    _, rows, width = shard_rows.shape
    vmem = pl.BlockSpec(memory_space=pltpu.VMEM)
    counts = [sum(n for _, n in pieces) for pieces in spans]
    return pl.pallas_call(
        functools.partial(pick_kernel, spans, len(after)),
        out_shape=[jax.ShapeDtypeStruct((n, rows, width), shard_rows.dtype) for n in counts],
        in_specs=[pl.BlockSpec(memory_space=pltpu.SMEM), vmem]
        + [pl.BlockSpec(memory_space=pl.ANY)] * len(after),
        out_specs=[vmem] * len(counts),
        compiler_params=pltpu.CompilerParams(vmem_limit_bytes=16 * MIB),
        cost_estimate=pl.CostEstimate(
            flops=0, bytes_accessed=2 * sum(counts) * rows * width * 2, transcendentals=0
        ),
    )(index, shard_rows, *after)


def times(a, b):
    return jnp.dot(
        a.astype(jnp.bfloat16), b.astype(jnp.bfloat16), preferred_element_type=jnp.float32
    )


def next_iterate(m):
    d = (times(m, m) - 10.0 * m) * (1.0 / 16.0)
    e = times(d, d) + 3.125 * d
    return (625.0 / 256.0) * m + times(e, m)


def root_of(stat):
    c = jnp.sqrt(jnp.sum(stat * stat))
    m0 = stat / c
    m1 = next_iterate(m0)
    m2 = next_iterate(m1)
    t = times(m0, m1)
    pair = m0 + m1
    total = times(5.0 * pair - t, m2) + 5.0 * t - 25.0 * (pair + m2)
    n = stat.shape[0]
    on_diagonal = lax.broadcasted_iota(jnp.int32, (n, n), 0) == lax.broadcasted_iota(
        jnp.int32, (n, n), 1
    )
    total = total + jnp.where(on_diagonal, 125.0, 0.0)
    return total * (lax.rsqrt(jnp.sqrt(c)) * (1.0 / 64.0))


def roots_kernel(owner_ref, refresh_ref, slot_ref, stat_ref, root_ref, out_ref):
    slot = slot_ref[0]

    def look(i, found):
        return found | jnp.where(owner_ref[refresh_ref[i]] == slot, 1, 0)

    fresh = lax.fori_loop(0, refresh_ref.shape[0], look, jnp.int32(0))

    @pl.when(fresh == 1)
    def _():
        out_ref[...] = root_of(stat_ref[...])

    @pl.when(fresh == 0)
    def _():
        out_ref[...] = root_ref[...]


def roots(owner_of, refresh, slot, stat, root):
    vmem = pl.BlockSpec(memory_space=pltpu.VMEM)
    smem = pl.BlockSpec(memory_space=pltpu.SMEM)
    return pl.pallas_call(
        roots_kernel,
        out_shape=jax.ShapeDtypeStruct(stat.shape, stat.dtype),
        in_specs=[smem, smem, smem, vmem, vmem],
        out_specs=vmem,
        compiler_params=pltpu.CompilerParams(vmem_limit_bytes=32 * MIB),
        cost_estimate=pl.CostEstimate(flops=8 * 2 * 512**3, bytes_accessed=3 * MIB, transcendentals=0),
    )(owner_of, refresh, slot, stat, root)


def finish_kernel(sources, n_owner, slot_ref, ls_ref, rs_ref, lr_ref, rr_ref, *refs):
    pieces, (up_ref, nl_ref, nr_ref, grad_ref) = refs[:-4], refs[-4:]
    owner = lax.rem(slot_ref[0], n_owner)
    z, y_hi, core = owner // 4, lax.rem(owner // 2, 2), lax.rem(owner, 2)
    n_z = n_owner // 4
    rows = pieces[0].shape[1]
    for piece, units in zip(pieces, sources):
        for i, (rz, yb, rc) in enumerate(units):
            z_from = lax.rem(z + (n_z - rz), n_z)
            y_from = 1 - y_hi if yb else y_hi
            core_from = 1 - core if rc else core
            row = pl.multiple_of((4 * z_from + 2 * y_from + core_from) * rows, rows)
            grad_ref[pl.ds(row, rows), :] = piece[i]
    grad = grad_ref[...]
    coeff = SHARE / grad.shape[1]
    f32 = jnp.float32
    left_part = jnp.dot(lr_ref[...].astype(jnp.bfloat16), grad, preferred_element_type=f32)
    up_ref[...] = jnp.dot(
        left_part.astype(jnp.bfloat16),
        rr_ref[...].astype(jnp.bfloat16),
        preferred_element_type=f32,
    ).astype(jnp.bfloat16)
    gram = lax.dot_general(grad, grad, (((1,), (1,)), ((), ())), preferred_element_type=f32)
    nl_ref[...] = DECAY * ls_ref[...] + coeff * gram
    gram = lax.dot_general(grad, grad, (((0,), (0,)), ((), ())), preferred_element_type=f32)
    nr_ref[...] = DECAY * rs_ref[...] + coeff * gram


def finish(slot, n_owner, pieces, sources, left_stat, right_stat, left_root, right_root):
    vmem = pl.BlockSpec(memory_space=pltpu.VMEM)
    smem = pl.BlockSpec(memory_space=pltpu.SMEM)
    return pl.pallas_call(
        functools.partial(finish_kernel, sources, n_owner),
        out_shape=[
            jax.ShapeDtypeStruct(left_stat.shape, jnp.bfloat16),
            jax.ShapeDtypeStruct(left_stat.shape, jnp.float32),
            jax.ShapeDtypeStruct(right_stat.shape, jnp.float32),
        ],
        in_specs=[smem] + [vmem] * (4 + len(pieces)),
        out_specs=[vmem] * 3,
        scratch_shapes=[pltpu.VMEM(left_stat.shape, jnp.bfloat16)],
        compiler_params=pltpu.CompilerParams(vmem_limit_bytes=32 * MIB),
        cost_estimate=pl.CostEstimate(flops=4 * 2 * 512**3, bytes_accessed=7 * MIB, transcendentals=0),
    )(slot, left_stat, right_stat, left_root, right_root, *pieces)


def plus(a, b):
    return (a.astype(jnp.float32) + b.astype(jnp.float32)).astype(jnp.bfloat16)


def per_device(grad_parts, owner_of, refresh, left_stat, right_stat, left_root, right_root):
    n_owner = lax.axis_size("owner")
    n_slots = lax.axis_size("dp") * n_owner
    my_slot = lax.axis_index("dp") * n_owner + lax.axis_index("owner")
    shard_rows = grad_parts[0]
    spans, table = build_table(n_slots, n_owner)
    mine = lax.dynamic_index_in_dim(jnp.asarray(table), my_slot, 0, keepdims=False)
    index = index_pieces(owner_of, mine)

    def send(x, **how):
        return lax.ppermute(x, AXES, route(n_slots, n_owner, **how))

    def step(name, number, x):
        orders = STREAMS[name][1]
        return lax.ppermute(x, AXES, route_step(n_slots, n_owner, orders, number))

    def rest(name, arrived, kept):
        for number in (1, 2):
            h = arrived.shape[0] // 2
            out = plus(arrived[h:], kept[h:])
            kept = plus(arrived[:h], kept[:h])
            arrived = step(name, number, out)
        return plus(arrived, kept)

    out = pick(index, shard_rows, [[spans["far", 1]], [spans["farthest", 1]]])
    far_in = step("far", 0, out[0])
    farthest_in = step("farthest", 0, out[1])
    ahead = pick(index, shard_rows, [[spans[("near", rz), 1], spans[("near", rz), 0]] for rz in (1, 7)])
    ahead = [send(p, rz=rz) for p, rz in zip(ahead, (1, 7))]
    kept = pick(
        index, shard_rows, [[spans[n, 0]] for n in ("far", "farthest", "middle", "here")]
    )
    middle_out, = pick(index, shard_rows, [[spans["middle", 1]]], after=(far_in, farthest_in))
    middle_in = step("middle", 0, middle_out)
    far = rest("far", far_in, kept[0])
    farthest = rest("farthest", farthest_in, kept[1])
    here_out, = pick(index, shard_rows, [[spans["here", 1]]], after=(middle_in,))
    here_in = step("here", 0, here_out)
    shape = (2, 2, 2, 4) + shard_rows.shape[1:]
    ahead = jnp.concatenate([p.reshape(shape) for p in ahead], axis=3)
    ahead = ahead.reshape((2, -1) + shard_rows.shape[1:])
    near_in = step("near", 0, ahead[0])
    middle = rest("middle", middle_in, kept[2])
    here = rest("here", here_in, kept[3])
    near = rest("near", near_in, ahead[1])

    travelled = [
        (3, send(far[:4], rz=3)),
        (5, send(far[4:], rz=5)),
        (4, send(farthest, rz=4)),
        (2, send(middle[:4], rz=2)),
        (6, send(middle[4:], rz=6)),
    ]
    at_home = [(0, here), (1, near[:4]), (7, near[4:])]
    pieces, sources = [], []
    for group in (travelled, at_home):
        for n, (yb, rc) in enumerate(QUAD):
            if (yb, rc) == (0, 0):
                for rz, x in group:
                    pieces.append(x[:1])
                    sources.append([(rz, yb, rc)])
                continue
            x = jnp.concatenate([x[n : n + 1] for _, x in group], axis=0)
            pieces.append(send(x, yb=yb, rc=rc))
            sources.append([(rz, yb, rc) for rz, _ in group])

    slot = my_slot.reshape(1)
    new_left_root = roots(owner_of, refresh, slot, left_stat[0], left_root[0])
    new_right_root = roots(owner_of, refresh, slot, right_stat[0], right_root[0])
    update, new_left, new_right = finish(
        slot, n_owner, pieces, sources, left_stat[0], right_stat[0], left_root[0], right_root[0]
    )
    return (
        update[None],
        new_left[None],
        new_right[None],
        new_left_root[None],
        new_right_root[None],
    )


def solution(mesh):
    owned = P(AXES, None, None)
    return jax.shard_map(
        per_device,
        mesh=mesh,
        in_specs=(P("dp", None, "owner", None), P(), P(), owned, owned, owned, owned),
        out_specs=(owned,) * 5,
        check_vma=False,
    )
```

time: 83.2 us -> 93.6 us (1.12)
  the two profiles are of different devices: /device:TPU:6 before, /device:TPU:1 now
where the time goes in v2:
time: 93.6 us; the launch traced here: 93.4 us
  starting transfers between devices  49.4 us (53%)
  waiting for transfers between devices  25.6 us (27%)
  Pallas kernels  11.8 us (13%)
  local copies, waits for them, and re-layouts  4.26 us (5%)
  other arithmetic  1.27 us (1%)
  between operations  1.07 us (1%)
    ppermute x13, starting transfers between devices, send(): return lax.ppermute(x, AXES, route(n_slots, n_owner, **how))  36.2 us
    ppermute x15, waiting for transfers between devices, step(): return lax.ppermute(x, AXES, route_step(n_slots, n_owner, orders, number))  19.1 us
    ppermute x15, starting transfers between devices, step(): return lax.ppermute(x, AXES, route_step(n_slots, n_owner, orders, number))  13.3 us
    ppermute x13, waiting for transfers between devices, send(): return lax.ppermute(x, AXES, route(n_slots, n_owner, **how))  6.47 us
    pallas_call x2, Pallas kernels, roots(): pl.pallas_call(roots_kernel, out_shape=jax.ShapeDtypeStruct(stat.shape, s...  3.83 us
    pallas_call x5, Pallas kernels, pick(): pl.pallas_call(functools.partial(pick_kernel, spans, len(after)), out_sha...  3.37 us
    unnamed x24, local copies, waits for them, and re-layouts  2.94 us
    pallas_call x1, Pallas kernels, finish(): pl.pallas_call(functools.partial(finish_kernel, sources, n_owner), out_sh...  2.41 us
  transfers between devices with their start and end apart: 28, of which 10 were waited for; matrix products, arithmetic and copies ran while one was open for 1% of the time, Pallas kernels for 7%

profile of v2, /device:TPU:1, one launch (start us, length us, event | category | flops | bytes accessed | tf_op | source)
XLA Modules:
  0.0 93.4 jit_solution(2645172256745139622)
XLA Ops:
  0.6 1.3 %constant_dynamic-slice_fusion = s32[1,256]{1,0:T(1,128)} fusion(s32[256,256]{1,0:T(8,128)} %constant.19.clone, s32[]{:T(128)S(6)} %select_n.4), kind=kLoop, calls=%fused_computation.52 | loop fusion | bytes 2052 | tf_op jit(solution)/shard_map/jit(dynamic_index_in_dim)/dynamic_slice | solution.py:245
  1.9 2.2 %shard_map.119.index_ref = s32[256]{0:T(256)} custom-call(s32[256]{0:T(256)} %owner_ref.5, s32[256]{0:T(256)} %bitcast.39), custom_call_target="tpu_custom_call" | custom-call | tf_op jit(solution)/shard_map/pallas_call | solution.py:93
  4.1 2.2 %copy-done = bf16[1,256,16,512]{3,2,1,0:T(8,128)(2,1)S(1)} copy-done((bf16[1,256,16,512]{3,2,1,0:T(8,128)(2,1)S(1)}, bf16[1,256,16,512]{3,2,1,0:T(8,128)(2,1)}, u32[]{:S(2)}) %copy-start) | copy-done | bytes 4194328
  7.7 3.4 %collective-permute-start = (bf16[32,16,512]{2,1,0:T(8,128)(2,1)S(1)}, bf16[32,16,512]{2,1,0:T(8,128)(2,1)S(1)}, u32[]{:S(2)}, u32[]{:S(2)}) collective-permute-start(bf16[32,16,512]{2,1,0:T(8,128)(2,1)S(1)} %get-tuple-element.16), channel_id=1, source_target_pairs={{0,64},{1,193},{2,66},{3,195},{4,68},{5,197},{6,70},{7,199},{8,72}... | collective-permute-start | bytes 1572872 | tf_op jit(solution)/shard_map/ppermute | solution.py:253
  11.1 1.3 %collective-permute-start.5 = (bf16[16,16,512]{2,1,0:T(8,128)(2,1)S(1)}, bf16[16,16,512]{2,1,0:T(8,128)(2,1)S(1)}, u32[]{:S(2)}, u32[]{:S(2)}) collective-permute-start(bf16[16,16,512]{2,1,0:T(8,128)(2,1)S(1)} %get-tuple-element.18), channel_id=1, source_target_pairs={{0,32},{1,33},{2,34},{3,35},{4,36},{5,37},{6,38},{7,39},{8,40},{9,... | collective-permute-start | bytes 786440 | tf_op jit(solution)/shard_map/ppermute | solution.py:253
  13.1 1.7 %collective-permute-start.20 = (bf16[32,16,512]{2,1,0:T(8,128)(2,1)S(1)}, bf16[32,16,512]{2,1,0:T(8,128)(2,1)S(1)}, u32[]{:S(2)}, u32[]{:S(2)}) collective-permute-start(bf16[32,16,512]{2,1,0:T(8,128)(2,1)S(1)} %get-tuple-element.22), channel_id=1, source_target_pairs={{0,4},{1,5},{2,6},{3,7},{4,8},{5,9},{6,10},{7,11},{8,12},{9,13},{1... | collective-permute-start | bytes 1572872 | tf_op jit(solution)/shard_map/ppermute | solution.py:249
  14.8 4.0 %collective-permute-start.21 = (bf16[32,16,512]{2,1,0:T(8,128)(2,1)S(1)}, bf16[32,16,512]{2,1,0:T(8,128)(2,1)S(1)}, u32[]{:S(2)}, u32[]{:S(2)}) collective-permute-start(bf16[32,16,512]{2,1,0:T(8,128)(2,1)S(1)} %get-tuple-element.23), channel_id=1, source_target_pairs={{0,28},{1,29},{2,30},{3,31},{4,0},{5,1},{6,2},{7,3},{8,4},{9,5},{1... | collective-permute-start | bytes 1572872 | tf_op jit(solution)/shard_map/ppermute | solution.py:249
  20.4 1.9 %shard_map.126 = f32[512,512]{1,0:T(8,128)} custom-call(s32[256]{0:T(256)S(1)} %copy-done.8, s32[32]{0:T(128)S(1)} %copy-done.9, s32[1]{0:T(128)} %bitcast.slot_ref, f32[512,512]{1,0:T(8,128)S(1)} %bitcast.26, f32[512,512]{1,0:T(8,128)S(1)} %bitcast.30), custom_call_target="tpu_custom_call" | custom-call | flops 2147483648 | bytes 3145728 | tf_op jit(solution)/shard_map/pallas_call | solution.py:179
  22.3 3.6 %collective-permute-done.6 = bf16[8,16,512]{2,1,0:T(8,128)(2,1)S(1)} collective-permute-done((bf16[8,16,512]{2,1,0:T(8,128)(2,1)S(1)}, bf16[8,16,512]{2,1,0:T(8,128)(2,1)S(1)}, u32[]{:S(2)}, u32[]{:S(2)}) %collective-permute-start.6) | collective-permute-done | bytes 131104 | tf_op jit(solution)/shard_map/ppermute | solution.py:253
  26.7 2.7 %collective-permute-done.7 = bf16[4,16,512]{2,1,0:T(8,128)(2,1)S(1)} collective-permute-done((bf16[4,16,512]{2,1,0:T(8,128)(2,1)S(1)}, bf16[4,16,512]{2,1,0:T(8,128)(2,1)S(1)}, u32[]{:S(2)}, u32[]{:S(2)}) %collective-permute-start.7) | collective-permute-done | bytes 65568 | tf_op jit(solution)/shard_map/ppermute | solution.py:253
  29.5 5.9 %collective-permute-start.8 = (bf16[4,16,512]{2,1,0:T(8,128)(2,1)S(1)}, bf16[4,16,512]{2,1,0:T(8,128)(2,1)S(1)}, u32[]{:S(2)}, u32[]{:S(2)}) collective-permute-start(bf16[4,16,512]{2,1,0:T(8,128)(2,1)S(1)} %add_convert_fusion.20), channel_id=1, source_target_pairs={{0,16},{1,17},{2,18},{3,19},{4,20},{5,21},{6,22},{7,23},{8,24},{9,... | collective-permute-start | bytes 196616 | tf_op jit(solution)/shard_map/ppermute | solution.py:249
  37.1 1.8 %collective-permute-start.9 = (bf16[32,16,512]{2,1,0:T(8,128)(2,1)S(1)}, bf16[32,16,512]{2,1,0:T(8,128)(2,1)S(1)}, u32[]{:S(2)}, u32[]{:S(2)}) collective-permute-start(bf16[32,16,512]{2,1,0:T(8,128)(2,1)S(1)} %shard_map.122), channel_id=1, source_target_pairs={{0,64},{1,193},{2,66},{3,195},{4,68},{5,197},{6,70},{7,199},{8,72}... | collective-permute-start | bytes 1572872 | tf_op jit(solution)/shard_map/ppermute | solution.py:253
  39.0 1.9 %collective-permute-start.3 = (bf16[4,16,512]{2,1,0:T(8,128)(2,1)S(1)}, bf16[4,16,512]{2,1,0:T(8,128)(2,1)S(1)}, u32[]{:S(2)}, u32[]{:S(2)}) collective-permute-start(bf16[4,16,512]{2,1,0:T(8,128)(2,1)S(1)} %get-tuple-element.50), channel_id=1, source_target_pairs={{0,12},{1,13},{2,14},{3,15},{4,16},{5,17},{6,18},{7,19},{8,20},{9,... | collective-permute-start | bytes 196616 | tf_op jit(solution)/shard_map/ppermute | solution.py:249
  41.0 2.7 %collective-permute-start.4 = (bf16[4,16,512]{2,1,0:T(8,128)(2,1)S(1)}, bf16[4,16,512]{2,1,0:T(8,128)(2,1)S(1)}, u32[]{:S(2)}, u32[]{:S(2)}) collective-permute-start(bf16[4,16,512]{2,1,0:T(8,128)(2,1)S(1)} %get-tuple-element.49), channel_id=1, source_target_pairs={{0,20},{1,21},{2,22},{3,23},{4,24},{5,25},{6,26},{7,27},{8,28},{9,... | collective-permute-start | bytes 196616 | tf_op jit(solution)/shard_map/ppermute | solution.py:249
  43.7 1.8 %collective-permute-done.3 = bf16[4,16,512]{2,1,0:T(8,128)(2,1)S(1)} collective-permute-done((bf16[4,16,512]{2,1,0:T(8,128)(2,1)S(1)}, bf16[4,16,512]{2,1,0:T(8,128)(2,1)S(1)}, u32[]{:S(2)}, u32[]{:S(2)}) %collective-permute-start.3) | collective-permute-done | bytes 65568 | tf_op jit(solution)/shard_map/ppermute | solution.py:249
  45.5 2.0 %collective-permute-done.4 = bf16[4,16,512]{2,1,0:T(8,128)(2,1)S(1)} collective-permute-done((bf16[4,16,512]{2,1,0:T(8,128)(2,1)S(1)}, bf16[4,16,512]{2,1,0:T(8,128)(2,1)S(1)}, u32[]{:S(2)}, u32[]{:S(2)}) %collective-permute-start.4) | collective-permute-done | bytes 65568 | tf_op jit(solution)/shard_map/ppermute | solution.py:249
  48.1 2.3 %collective-permute-done.9.refs_0_ = bf16[32,16,512]{2,1,0:T(8,128)(2,1)S(1)} collective-permute-done((bf16[32,16,512]{2,1,0:T(8,128)(2,1)S(1)}, bf16[32,16,512]{2,1,0:T(8,128)(2,1)S(1)}, u32[]{:S(2)}, u32[]{:S(2)}) %collective-permute-start.9) | collective-permute-done | bytes 524320 | tf_op jit(solution)/shard_map/ppermute | solution.py:253
  51.0 1.4 %collective-permute-start.17 = (bf16[16,16,512]{2,1,0:T(8,128)(2,1)S(1)}, bf16[16,16,512]{2,1,0:T(8,128)(2,1)S(1)}, u32[]{:S(2)}, u32[]{:S(2)}) collective-permute-start(bf16[16,16,512]{2,1,0:T(8,128)(2,1)S(1)} %shard_map.123), channel_id=1, source_target_pairs={{0,32},{1,33},{2,34},{3,35},{4,36},{5,37},{6,38},{7,39},{8,40},{9,... | collective-permute-start | bytes 786440 | tf_op jit(solution)/shard_map/ppermute | solution.py:253
  52.7 2.9 %collective-permute-done.23 = bf16[16,16,512]{2,1,0:T(8,128)(2,1)S(1)} collective-permute-done((bf16[16,16,512]{2,1,0:T(8,128)(2,1)S(1)}, bf16[16,16,512]{2,1,0:T(8,128)(2,1)S(1)}, u32[]{:S(2)}, u32[]{:S(2)}) %collective-permute-start.23) | collective-permute-done | bytes 262176 | tf_op jit(solution)/shard_map/ppermute | solution.py:253
  55.6 1.4 %collective-permute-start.24 = (bf16[8,16,512]{2,1,0:T(8,128)(2,1)S(1)}, bf16[8,16,512]{2,1,0:T(8,128)(2,1)S(1)}, u32[]{:S(2)}, u32[]{:S(2)}) collective-permute-start(bf16[8,16,512]{2,1,0:T(8,128)(2,1)S(1)} %add_convert_fusion.6), channel_id=1, source_target_pairs={{0,192},{1,33},{2,194},{3,35},{4,196},{5,37},{6,198},{7,39},{8,200... | collective-permute-start | bytes 393224 | tf_op jit(solution)/shard_map/ppermute | solution.py:253
  57.0 2.2 %collective-permute-done.17 = bf16[16,16,512]{2,1,0:T(8,128)(2,1)S(1)} collective-permute-done((bf16[16,16,512]{2,1,0:T(8,128)(2,1)S(1)}, bf16[16,16,512]{2,1,0:T(8,128)(2,1)S(1)}, u32[]{:S(2)}, u32[]{:S(2)}) %collective-permute-start.17) | collective-permute-done | bytes 262176 | tf_op jit(solution)/shard_map/ppermute | solution.py:253
  59.3 1.2 %collective-permute-start.18 = (bf16[8,16,512]{2,1,0:T(8,128)(2,1)S(1)}, bf16[8,16,512]{2,1,0:T(8,128)(2,1)S(1)}, u32[]{:S(2)}, u32[]{:S(2)}) collective-permute-start(bf16[8,16,512]{2,1,0:T(8,128)(2,1)S(1)} %get-tuple-element.35), channel_id=1, source_target_pairs={{0,192},{1,193},{2,194},{3,195},{4,196},{5,197},{6,198},{7,199},{8... | collective-permute-start | bytes 393224 | tf_op jit(solution)/shard_map/ppermute | solution.py:253
  60.8 4.1 %collective-permute-done.18 = bf16[8,16,512]{2,1,0:T(8,128)(2,1)S(1)} collective-permute-done((bf16[8,16,512]{2,1,0:T(8,128)(2,1)S(1)}, bf16[8,16,512]{2,1,0:T(8,128)(2,1)S(1)}, u32[]{:S(2)}, u32[]{:S(2)}) %collective-permute-start.18) | collective-permute-done | bytes 131104 | tf_op jit(solution)/shard_map/ppermute | solution.py:253
  65.0 1.3 %collective-permute-done.11 = bf16[8,16,512]{2,1,0:T(8,128)(2,1)S(1)} collective-permute-done((bf16[8,16,512]{2,1,0:T(8,128)(2,1)S(1)}, bf16[8,16,512]{2,1,0:T(8,128)(2,1)S(1)}, u32[]{:S(2)}, u32[]{:S(2)}) %collective-permute-start.11) | collective-permute-done | bytes 131104 | tf_op jit(solution)/shard_map/ppermute | solution.py:253
  66.5 1.2 %collective-permute-start.12 = (bf16[4,16,512]{2,1,0:T(8,128)(2,1)S(1)}, bf16[4,16,512]{2,1,0:T(8,128)(2,1)S(1)}, u32[]{:S(2)}, u32[]{:S(2)}) collective-permute-start(bf16[4,16,512]{2,1,0:T(8,128)(2,1)S(1)} %get-tuple-element.48), channel_id=1, source_target_pairs={{0,8},{1,9},{2,10},{3,11},{4,12},{5,13},{6,14},{7,15},{8,16},{9,17... | collective-permute-start | bytes 196616 | tf_op jit(solution)/shard_map/ppermute | solution.py:249
  67.7 2.4 %collective-permute-start.13 = (bf16[4,16,512]{2,1,0:T(8,128)(2,1)S(1)}, bf16[4,16,512]{2,1,0:T(8,128)(2,1)S(1)}, u32[]{:S(2)}, u32[]{:S(2)}) collective-permute-start(bf16[4,16,512]{2,1,0:T(8,128)(2,1)S(1)} %get-tuple-element.47), channel_id=1, source_target_pairs={{0,24},{1,25},{2,26},{3,27},{4,28},{5,29},{6,30},{7,31},{8,0},{9,1... | collective-permute-start | bytes 196616 | tf_op jit(solution)/shard_map/ppermute | solution.py:249
  70.2 11.5 %collective-permute-start.27 = (bf16[3,16,512]{2,1,0:T(8,128)(2,1)S(1)}, bf16[3,16,512]{2,1,0:T(8,128)(2,1)S(1)}, u32[]{:S(2)}, u32[]{:S(2)}) collective-permute-start(bf16[3,16,512]{2,1,0:T(8,128)(2,1)S(1)} %pad_maximum_fusion.3), channel_id=1, source_target_pairs={{0,35},{1,34},{2,33},{3,32},{4,39},{5,38},{6,37},{7,36},{8,43},{9,... | collective-permute-start | bytes 147464 | tf_op jit(solution)/shard_map/ppermute | solution.py:249
  82.6 2.8 %collective-permute-start.15 = (bf16[5,16,512]{2,1,0:T(8,128)(2,1)S(1)}, bf16[5,16,512]{2,1,0:T(8,128)(2,1)S(1)}, u32[]{:S(2)}, u32[]{:S(2)}) collective-permute-start(bf16[5,16,512]{2,1,0:T(8,128)(2,1)S(1)} %get-tuple-element.56), channel_id=1, source_target_pairs={{0,34},{1,35},{2,32},{3,33},{4,38},{5,39},{6,36},{7,37},{8,42},{9,... | collective-permute-start | bytes 245768 | tf_op jit(solution)/shard_map/ppermute | solution.py:249
  85.4 1.1 %collective-permute-start.16 = (bf16[5,16,512]{2,1,0:T(8,128)(2,1)S(1)}, bf16[5,16,512]{2,1,0:T(8,128)(2,1)S(1)}, u32[]{:S(2)}, u32[]{:S(2)}) collective-permute-start(bf16[5,16,512]{2,1,0:T(8,128)(2,1)S(1)} %get-tuple-element.55), channel_id=1, source_target_pairs={{0,35},{1,34},{2,33},{3,32},{4,39},{5,38},{6,37},{7,36},{8,43},{9,... | collective-permute-start | bytes 245768 | tf_op jit(solution)/shard_map/ppermute | solution.py:249
  86.5 1.9 %shard_map.127 = f32[512,512]{1,0:T(8,128)} custom-call(s32[256]{0:T(256)S(1)} %copy-done.8, s32[32]{0:T(128)S(1)} %copy-done.9, s32[1]{0:T(128)} %bitcast.slot_ref, f32[512,512]{1,0:T(8,128)S(1)} %bitcast.28, f32[512,512]{1,0:T(8,128)S(1)} %bitcast.32), custom_call_target="tpu_custom_call" | custom-call | flops 2147483648 | bytes 3145728 | tf_op jit(solution)/shard_map/pallas_call | solution.py:179
  88.4 2.6 %collective-permute-done.16.refs_7_ = bf16[5,16,512]{2,1,0:T(8,128)(2,1)S(1)} collective-permute-done((bf16[5,16,512]{2,1,0:T(8,128)(2,1)S(1)}, bf16[5,16,512]{2,1,0:T(8,128)(2,1)S(1)}, u32[]{:S(2)}, u32[]{:S(2)}) %collective-permute-start.16) | collective-permute-done | bytes 81952 | tf_op jit(solution)/shard_map/ppermute | solution.py:249
  91.0 2.4 %shard_map.125 = (bf16[512,512]{1,0:T(8,128)(2,1)}, f32[512,512]{1,0:T(8,128)}, f32[512,512]{1,0:T(8,128)}) custom-call(s32[1]{0:T(128)} %bitcast.slot_ref, f32[512,512]{1,0:T(8,128)S(1)} %bitcast.27, f32[512,512]{1,0:T(8,128)S(1)} %bitcast.29, f32[512,512]{1,0:T(8,128)S(1)} %bitcast.31, f32[512,512]{1,0:T(8,128)S(1)} %bitcast.33, ...), custom_call_target="tpu_custom_call" | custom-call | flops 1073741824 | bytes 7340032 | tf_op jit(solution)/shard_map/pallas_call | solution.py:220
  (83 shorter events, 9.0 us)
Async XLA Ops:
  7.7 12.4 %collective-permute-start = (bf16[32,16,512]{2,1,0:T(8,128)(2,1)S(1)}, bf16[32,16,512]{2,1,0:T(8,128)(2,1)S(1)}, u32[]{:S(2)}, u32[]{:S(2)}) collective-permute-start(bf16[32,16,512]{2,1,0:T(8,128)(2,1)S(1)} %get-tuple-element.16), channel_id=1, source_target_pairs={{0,64},{1,193},{2,66},{3,195},{4,68},{5,197},{6,70},{7,199},{8,72}... | collective-permute-start | bytes 1572872 | tf_op jit(solution)/shard_map/ppermute | solution.py:253
  11.1 8.6 %collective-permute-start.5 = (bf16[16,16,512]{2,1,0:T(8,128)(2,1)S(1)}, bf16[16,16,512]{2,1,0:T(8,128)(2,1)S(1)}, u32[]{:S(2)}, u32[]{:S(2)}) collective-permute-start(bf16[16,16,512]{2,1,0:T(8,128)(2,1)S(1)} %get-tuple-element.18), channel_id=1, source_target_pairs={{0,32},{1,33},{2,34},{3,35},{4,36},{5,37},{6,38},{7,39},{8,40},{9,... | collective-permute-start | bytes 786440 | tf_op jit(solution)/shard_map/ppermute | solution.py:253
  13.1 22.3 %collective-permute-start.20 = (bf16[32,16,512]{2,1,0:T(8,128)(2,1)S(1)}, bf16[32,16,512]{2,1,0:T(8,128)(2,1)S(1)}, u32[]{:S(2)}, u32[]{:S(2)}) collective-permute-start(bf16[32,16,512]{2,1,0:T(8,128)(2,1)S(1)} %get-tuple-element.22), channel_id=1, source_target_pairs={{0,4},{1,5},{2,6},{3,7},{4,8},{5,9},{6,10},{7,11},{8,12},{9,13},{1... | collective-permute-start | bytes 1572872 | tf_op jit(solution)/shard_map/ppermute | solution.py:249
  14.8 20.6 %collective-permute-start.21 = (bf16[32,16,512]{2,1,0:T(8,128)(2,1)S(1)}, bf16[32,16,512]{2,1,0:T(8,128)(2,1)S(1)}, u32[]{:S(2)}, u32[]{:S(2)}) collective-permute-start(bf16[32,16,512]{2,1,0:T(8,128)(2,1)S(1)} %get-tuple-element.23), channel_id=1, source_target_pairs={{0,28},{1,29},{2,30},{3,31},{4,0},{5,1},{6,2},{7,3},{8,4},{9,5},{1... | collective-permute-start | bytes 1572872 | tf_op jit(solution)/shard_map/ppermute | solution.py:249
  19.8 6.1 %collective-permute-start.6 = (bf16[8,16,512]{2,1,0:T(8,128)(2,1)S(1)}, bf16[8,16,512]{2,1,0:T(8,128)(2,1)S(1)}, u32[]{:S(2)}, u32[]{:S(2)}) collective-permute-start(bf16[8,16,512]{2,1,0:T(8,128)(2,1)S(1)} %get-tuple-element.37), channel_id=1, source_target_pairs={{0,192},{1,193},{2,194},{3,195},{4,196},{5,197},{6,198},{7,199},{8... | collective-permute-start | bytes 393224 | tf_op jit(solution)/shard_map/ppermute | solution.py:253
  20.3 5.8 %collective-permute-start.1 = (bf16[16,16,512]{2,1,0:T(8,128)(2,1)S(1)}, bf16[16,16,512]{2,1,0:T(8,128)(2,1)S(1)}, u32[]{:S(2)}, u32[]{:S(2)}) collective-permute-start(bf16[16,16,512]{2,1,0:T(8,128)(2,1)S(1)} %get-tuple-element.31), channel_id=1, source_target_pairs={{0,32},{1,65},{2,34},{3,67},{4,36},{5,69},{6,38},{7,71},{8,40},{9,... | collective-permute-start | bytes 786440 | tf_op jit(solution)/shard_map/ppermute | solution.py:253
  20.4 16.1 %copy-start.1 = (bf16[1,256,16,512]{3,2,1,0:T(8,128)(2,1)S(1)}, bf16[1,256,16,512]{3,2,1,0:T(8,128)(2,1)}, u32[]{:S(2)}) copy-start(bf16[1,256,16,512]{3,2,1,0:T(8,128)(2,1)} %param.8) | copy-start | bytes 12582916
  20.4 16.1 %copy-start.7 = (s32[256]{0:T(256)S(1)}, s32[256]{0:T(256)}, u32[]{:S(2)}) copy-start(s32[256]{0:T(256)} %shard_map.119.index_ref) | copy-start | bytes 3076
  25.9 3.5 %collective-permute-start.7 = (bf16[4,16,512]{2,1,0:T(8,128)(2,1)S(1)}, bf16[4,16,512]{2,1,0:T(8,128)(2,1)S(1)}, u32[]{:S(2)}, u32[]{:S(2)}) collective-permute-start(bf16[4,16,512]{2,1,0:T(8,128)(2,1)S(1)} %add_convert_fusion.22), channel_id=1, source_target_pairs={{0,64},{1,65},{2,66},{3,67},{4,68},{5,69},{6,70},{7,71},{8,72},{9,... | collective-permute-start | bytes 196616 | tf_op jit(solution)/shard_map/ppermute | solution.py:253
  26.1 12.9 %collective-permute-start.2 = (bf16[8,16,512]{2,1,0:T(8,128)(2,1)S(1)}, bf16[8,16,512]{2,1,0:T(8,128)(2,1)S(1)}, u32[]{:S(2)}, u32[]{:S(2)}) collective-permute-start(bf16[8,16,512]{2,1,0:T(8,128)(2,1)S(1)} %add_convert_fusion.16), channel_id=1, source_target_pairs={{0,192},{1,33},{2,194},{3,35},{4,196},{5,37},{6,198},{7,39},{8,200... | collective-permute-start | bytes 393224 | tf_op jit(solution)/shard_map/ppermute | solution.py:253
  29.5 18.6 %collective-permute-start.8 = (bf16[4,16,512]{2,1,0:T(8,128)(2,1)S(1)}, bf16[4,16,512]{2,1,0:T(8,128)(2,1)S(1)}, u32[]{:S(2)}, u32[]{:S(2)}) collective-permute-start(bf16[4,16,512]{2,1,0:T(8,128)(2,1)S(1)} %add_convert_fusion.20), channel_id=1, source_target_pairs={{0,16},{1,17},{2,18},{3,19},{4,20},{5,21},{6,22},{7,23},{8,24},{9,... | collective-permute-start | bytes 196616 | tf_op jit(solution)/shard_map/ppermute | solution.py:249
  35.5 12.1 %collective-permute-start.22 = (bf16[32,16,512]{2,1,0:T(8,128)(2,1)S(1)}, bf16[32,16,512]{2,1,0:T(8,128)(2,1)S(1)}, u32[]{:S(2)}, u32[]{:S(2)}) collective-permute-start(bf16[32,16,512]{2,1,0:T(8,128)(2,1)S(1)} %bitcast.38), channel_id=1, source_target_pairs={{0,64},{1,193},{2,66},{3,195},{4,68},{5,197},{6,70},{7,199},{8,72}... | collective-permute-start | bytes 1572872 | tf_op jit(solution)/shard_map/ppermute | solution.py:253
  37.1 13.3 %collective-permute-start.9 = (bf16[32,16,512]{2,1,0:T(8,128)(2,1)S(1)}, bf16[32,16,512]{2,1,0:T(8,128)(2,1)S(1)}, u32[]{:S(2)}, u32[]{:S(2)}) collective-permute-start(bf16[32,16,512]{2,1,0:T(8,128)(2,1)S(1)} %shard_map.122), channel_id=1, source_target_pairs={{0,64},{1,193},{2,66},{3,195},{4,68},{5,197},{6,70},{7,199},{8,72}... | collective-permute-start | bytes 1572872 | tf_op jit(solution)/shard_map/ppermute | solution.py:253
  39.0 6.5 %collective-permute-start.3 = (bf16[4,16,512]{2,1,0:T(8,128)(2,1)S(1)}, bf16[4,16,512]{2,1,0:T(8,128)(2,1)S(1)}, u32[]{:S(2)}, u32[]{:S(2)}) collective-permute-start(bf16[4,16,512]{2,1,0:T(8,128)(2,1)S(1)} %get-tuple-element.50), channel_id=1, source_target_pairs={{0,12},{1,13},{2,14},{3,15},{4,16},{5,17},{6,18},{7,19},{8,20},{9,... | collective-permute-start | bytes 196616 | tf_op jit(solution)/shard_map/ppermute | solution.py:249
  41.0 6.5 %collective-permute-start.4 = (bf16[4,16,512]{2,1,0:T(8,128)(2,1)S(1)}, bf16[4,16,512]{2,1,0:T(8,128)(2,1)S(1)}, u32[]{:S(2)}, u32[]{:S(2)}) collective-permute-start(bf16[4,16,512]{2,1,0:T(8,128)(2,1)S(1)} %get-tuple-element.49), channel_id=1, source_target_pairs={{0,20},{1,21},{2,22},{3,23},{4,24},{5,25},{6,26},{7,27},{8,28},{9,... | collective-permute-start | bytes 196616 | tf_op jit(solution)/shard_map/ppermute | solution.py:249
  47.8 7.8 %collective-permute-start.23 = (bf16[16,16,512]{2,1,0:T(8,128)(2,1)S(1)}, bf16[16,16,512]{2,1,0:T(8,128)(2,1)S(1)}, u32[]{:S(2)}, u32[]{:S(2)}) collective-permute-start(bf16[16,16,512]{2,1,0:T(8,128)(2,1)S(1)} %get-tuple-element.33), channel_id=1, source_target_pairs={{0,32},{1,65},{2,34},{3,67},{4,36},{5,69},{6,38},{7,71},{8,40},{9,... | collective-permute-start | bytes 786440 | tf_op jit(solution)/shard_map/ppermute | solution.py:253
  51.0 35.5 %copy-start.3 = (f32[1,512,512]{2,1,0:T(8,128)S(1)}, f32[1,512,512]{2,1,0:T(8,128)}, u32[]{:S(2)}) copy-start(f32[1,512,512]{2,1,0:T(8,128)} %param.12) | copy-start | bytes 3145732
  51.0 35.5 %copy-start.5 = (f32[1,512,512]{2,1,0:T(8,128)S(1)}, f32[1,512,512]{2,1,0:T(8,128)}, u32[]{:S(2)}) copy-start(f32[1,512,512]{2,1,0:T(8,128)} %param.14) | copy-start | bytes 3145732
  51.0 8.2 %collective-permute-start.17 = (bf16[16,16,512]{2,1,0:T(8,128)(2,1)S(1)}, bf16[16,16,512]{2,1,0:T(8,128)(2,1)S(1)}, u32[]{:S(2)}, u32[]{:S(2)}) collective-permute-start(bf16[16,16,512]{2,1,0:T(8,128)(2,1)S(1)} %shard_map.123), channel_id=1, source_target_pairs={{0,32},{1,33},{2,34},{3,35},{4,36},{5,37},{6,38},{7,39},{8,40},{9,... | collective-permute-start | bytes 786440 | tf_op jit(solution)/shard_map/ppermute | solution.py:253
  52.6 8.0 %collective-permute-start.10 = (bf16[16,16,512]{2,1,0:T(8,128)(2,1)S(1)}, bf16[16,16,512]{2,1,0:T(8,128)(2,1)S(1)}, u32[]{:S(2)}, u32[]{:S(2)}) collective-permute-start(bf16[16,16,512]{2,1,0:T(8,128)(2,1)S(1)} %get-tuple-element.29), channel_id=1, source_target_pairs={{0,32},{1,65},{2,34},{3,67},{4,36},{5,69},{6,38},{7,71},{8,40},{9,... | collective-permute-start | bytes 786440 | tf_op jit(solution)/shard_map/ppermute | solution.py:253
  55.6 10.8 %collective-permute-start.24 = (bf16[8,16,512]{2,1,0:T(8,128)(2,1)S(1)}, bf16[8,16,512]{2,1,0:T(8,128)(2,1)S(1)}, u32[]{:S(2)}, u32[]{:S(2)}) collective-permute-start(bf16[8,16,512]{2,1,0:T(8,128)(2,1)S(1)} %add_convert_fusion.6), channel_id=1, source_target_pairs={{0,192},{1,33},{2,194},{3,35},{4,196},{5,37},{6,198},{7,39},{8,200... | collective-permute-start | bytes 393224 | tf_op jit(solution)/shard_map/ppermute | solution.py:253
  59.3 5.6 %collective-permute-start.18 = (bf16[8,16,512]{2,1,0:T(8,128)(2,1)S(1)}, bf16[8,16,512]{2,1,0:T(8,128)(2,1)S(1)}, u32[]{:S(2)}, u32[]{:S(2)}) collective-permute-start(bf16[8,16,512]{2,1,0:T(8,128)(2,1)S(1)} %get-tuple-element.35), channel_id=1, source_target_pairs={{0,192},{1,193},{2,194},{3,195},{4,196},{5,197},{6,198},{7,199},{8... | collective-permute-start | bytes 393224 | tf_op jit(solution)/shard_map/ppermute | solution.py:253
  60.6 5.7 %collective-permute-start.11 = (bf16[8,16,512]{2,1,0:T(8,128)(2,1)S(1)}, bf16[8,16,512]{2,1,0:T(8,128)(2,1)S(1)}, u32[]{:S(2)}, u32[]{:S(2)}) collective-permute-start(bf16[8,16,512]{2,1,0:T(8,128)(2,1)S(1)} %add_convert_fusion.11), channel_id=1, source_target_pairs={{0,192},{1,33},{2,194},{3,35},{4,196},{5,37},{6,198},{7,39},{8,200... | collective-permute-start | bytes 393224 | tf_op jit(solution)/shard_map/ppermute | solution.py:253
  64.9 5.2 %collective-permute-start.19 = (bf16[4,16,512]{2,1,0:T(8,128)(2,1)S(1)}, bf16[4,16,512]{2,1,0:T(8,128)(2,1)S(1)}, u32[]{:S(2)}, u32[]{:S(2)}) collective-permute-start(bf16[4,16,512]{2,1,0:T(8,128)(2,1)S(1)} %add_convert_fusion.19), channel_id=1, source_target_pairs={{0,64},{1,65},{2,66},{3,67},{4,68},{5,69},{6,70},{7,71},{8,72},{9,... | collective-permute-start | bytes 196616 | tf_op jit(solution)/shard_map/ppermute | solution.py:253
  66.5 15.9 %collective-permute-start.12 = (bf16[4,16,512]{2,1,0:T(8,128)(2,1)S(1)}, bf16[4,16,512]{2,1,0:T(8,128)(2,1)S(1)}, u32[]{:S(2)}, u32[]{:S(2)}) collective-permute-start(bf16[4,16,512]{2,1,0:T(8,128)(2,1)S(1)} %get-tuple-element.48), channel_id=1, source_target_pairs={{0,8},{1,9},{2,10},{3,11},{4,12},{5,13},{6,14},{7,15},{8,16},{9,17... | collective-permute-start | bytes 196616 | tf_op jit(solution)/shard_map/ppermute | solution.py:249
  67.7 14.7 %collective-permute-start.13 = (bf16[4,16,512]{2,1,0:T(8,128)(2,1)S(1)}, bf16[4,16,512]{2,1,0:T(8,128)(2,1)S(1)}, u32[]{:S(2)}, u32[]{:S(2)}) collective-permute-start(bf16[4,16,512]{2,1,0:T(8,128)(2,1)S(1)} %get-tuple-element.47), channel_id=1, source_target_pairs={{0,24},{1,25},{2,26},{3,27},{4,28},{5,29},{6,30},{7,31},{8,0},{9,1... | collective-permute-start | bytes 196616 | tf_op jit(solution)/shard_map/ppermute | solution.py:249
  70.2 15.2 %collective-permute-start.27 = (bf16[3,16,512]{2,1,0:T(8,128)(2,1)S(1)}, bf16[3,16,512]{2,1,0:T(8,128)(2,1)S(1)}, u32[]{:S(2)}, u32[]{:S(2)}) collective-permute-start(bf16[3,16,512]{2,1,0:T(8,128)(2,1)S(1)} %pad_maximum_fusion.3), channel_id=1, source_target_pairs={{0,35},{1,34},{2,33},{3,32},{4,39},{5,38},{6,37},{7,36},{8,43},{9,... | collective-permute-start | bytes 147464 | tf_op jit(solution)/shard_map/ppermute | solution.py:249
  81.7 6.6 %collective-permute-start.26 = (bf16[3,16,512]{2,1,0:T(8,128)(2,1)S(1)}, bf16[3,16,512]{2,1,0:T(8,128)(2,1)S(1)}, u32[]{:S(2)}, u32[]{:S(2)}) collective-permute-start(bf16[3,16,512]{2,1,0:T(8,128)(2,1)S(1)} %pad_maximum_fusion.2), channel_id=1, source_target_pairs={{0,34},{1,35},{2,32},{3,33},{4,38},{5,39},{6,36},{7,37},{8,42},{9,... | collective-permute-start | bytes 147464 | tf_op jit(solution)/shard_map/ppermute | solution.py:249
  81.9 6.5 %collective-permute-start.25 = (bf16[3,16,512]{2,1,0:T(8,128)(2,1)S(1)}, bf16[3,16,512]{2,1,0:T(8,128)(2,1)S(1)}, u32[]{:S(2)}, u32[]{:S(2)}) collective-permute-start(bf16[3,16,512]{2,1,0:T(8,128)(2,1)S(1)} %pad_maximum_fusion.1), channel_id=1, source_target_pairs={{0,1},{1,0},{2,3},{3,2},{4,5},{5,4},{6,7},{7,6},{8,9},{9,8},{10,11... | collective-permute-start | bytes 147464 | tf_op jit(solution)/shard_map/ppermute | solution.py:249
  82.4 6.0 %collective-permute-start.14 = (bf16[5,16,512]{2,1,0:T(8,128)(2,1)S(1)}, bf16[5,16,512]{2,1,0:T(8,128)(2,1)S(1)}, u32[]{:S(2)}, u32[]{:S(2)}) collective-permute-start(bf16[5,16,512]{2,1,0:T(8,128)(2,1)S(1)} %get-tuple-element.57), channel_id=1, source_target_pairs={{0,1},{1,0},{2,3},{3,2},{4,5},{5,4},{6,7},{7,6},{8,9},{9,8},{10,11... | collective-permute-start | bytes 245768 | tf_op jit(solution)/shard_map/ppermute | solution.py:249
  82.6 5.8 %collective-permute-start.15 = (bf16[5,16,512]{2,1,0:T(8,128)(2,1)S(1)}, bf16[5,16,512]{2,1,0:T(8,128)(2,1)S(1)}, u32[]{:S(2)}, u32[]{:S(2)}) collective-permute-start(bf16[5,16,512]{2,1,0:T(8,128)(2,1)S(1)} %get-tuple-element.56), channel_id=1, source_target_pairs={{0,34},{1,35},{2,32},{3,33},{4,38},{5,39},{6,36},{7,37},{8,42},{9,... | collective-permute-start | bytes 245768 | tf_op jit(solution)/shard_map/ppermute | solution.py:249
  85.4 5.6 %collective-permute-start.16 = (bf16[5,16,512]{2,1,0:T(8,128)(2,1)S(1)}, bf16[5,16,512]{2,1,0:T(8,128)(2,1)S(1)}, u32[]{:S(2)}, u32[]{:S(2)}) collective-permute-start(bf16[5,16,512]{2,1,0:T(8,128)(2,1)S(1)} %get-tuple-element.55), channel_id=1, source_target_pairs={{0,35},{1,34},{2,33},{3,32},{4,39},{5,38},{6,37},{7,36},{8,43},{9,... | collective-permute-start | bytes 245768 | tf_op jit(solution)/shard_map/ppermute | solution.py:249
  (6 other events, 32.0 us)

commit v3 on v1

v3 whole, which is shorter than its diff:
```python
import functools

import jax
import jax.numpy as jnp
import numpy as np
from jax import lax
from jax.experimental import pallas as pl
from jax.experimental.pallas import tpu as pltpu
from jax.sharding import PartitionSpec as P

DECAY = 0.9
SHARE = 0.1
AXES = ("dp", "owner")
MIB = 1 << 20
CHUNKS = 8
MOST_MIB = 61

WIDE, SLIM = {0: "ayb", 1: "bay"}, {0: "yba", 1: "yba"}
X_OF, Y_OF = {"a": 1, "b": 3, "y": 0}, {"a": 0, "b": 0, "y": 1}


def build_streams(n_owner):
    cut = -(-2 * n_owner // 3)
    return [(0, cut, WIDE), (cut, n_owner - cut, SLIM)]


def route(n_slots, n_owner, orders, step):
    pairs = []
    for s in range(n_slots):
        data, owner = divmod(s, n_owner)
        dim = orders[owner % 2][step]
        to = (data // 2 ^ X_OF[dim]) * 2 + (data % 2 ^ Y_OF[dim])
        pairs.append((s, to * n_owner + owner))
    return pairs


def pick_kernel(groups, n_owner, chunks, n_after, slot_ref, owner_ref, shard_ref, *refs):
    outs, token = refs[n_after : n_after + len(groups)], refs[n_after + len(groups)]
    block_at, owners, sem = refs[n_after + len(groups) + 1 :][:3]
    copies = []
    if chunks:
        held, sems = refs[-2:]
        n = shard_ref.shape[0] // chunks
        for k in range(chunks):
            part = pl.ds(k * n, n)
            copies.append(pltpu.make_async_copy(shard_ref.at[part], held.at[part], sems.at[k]))
    else:
        held = shard_ref
    read_owners = pltpu.make_async_copy(owner_ref, owners, sem)
    read_owners.start()
    for copy in copies:
        copy.start()
    token[...] = jnp.zeros_like(token)
    slot = slot_ref[0]
    data, core = slot // n_owner, lax.rem(slot, 2)
    x, y_lo = data // 2, lax.rem(data, 2)
    read_owners.wait()

    @pl.loop(0, owners.shape[0], unroll=8)
    def _(b):
        block_at[owners[b]] = b

    for copy in copies:
        copy.wait()
    for out, (begin, count, orders, first) in zip(outs, groups):
        for second in (0, 1):
            for third in (0, 1):
                bits = (first, second, third)
                on_x, on_y = [0, 0], [0, 0]
                for c in (0, 1):
                    for dim, bit in zip(orders[c], (first, second, third)):
                        on_x[c] ^= X_OF[dim] * bit
                        on_y[c] ^= Y_OF[dim] * bit
                to_x = x ^ jnp.where(core == 0, on_x[0], on_x[1])
                to_y = y_lo ^ jnp.where(core == 0, on_y[0], on_y[1])
                base = (to_x * 2 + to_y) * n_owner + begin
                offset = (2 * second + third) * count

                @pl.loop(0, count, unroll=max(d for d in range(1, 12) if count % d == 0))
                def _(i, out=out, offset=offset, base=base):
                    out[offset + i] = held[block_at[base + i]]


def pick(slot, n_owner, owner_of, shard_rows, groups, after=(), chunks=0):
    _, rows, width = shard_rows.shape
    vmem = pl.BlockSpec(memory_space=pltpu.VMEM)
    smem = pl.BlockSpec(memory_space=pltpu.SMEM)
    anywhere = pl.BlockSpec(memory_space=pl.ANY)
    scratch = [
        pltpu.SMEM(owner_of.shape, jnp.int32),
        pltpu.SMEM(owner_of.shape, jnp.int32),
        pltpu.SemaphoreType.DMA,
    ]
    if chunks:
        scratch += [
            pltpu.VMEM(shard_rows.shape, shard_rows.dtype),
            pltpu.SemaphoreType.DMA((chunks,)),
        ]
    return pl.pallas_call(
        functools.partial(pick_kernel, groups, n_owner, chunks, len(after)),
        out_shape=[
            jax.ShapeDtypeStruct((4 * count, rows, width), shard_rows.dtype)
            for _, count, _, _ in groups
        ]
        + [jax.ShapeDtypeStruct((8, 128), jnp.float32)],
        in_specs=[smem, anywhere, anywhere if chunks else vmem] + [anywhere] * len(after),
        out_specs=[vmem] * (len(groups) + 1),
        scratch_shapes=scratch,
        compiler_params=pltpu.CompilerParams(vmem_limit_bytes=(MOST_MIB if chunks else 16) * MIB),
        cost_estimate=pl.CostEstimate(flops=0, bytes_accessed=1024, transcendentals=0),
    )(slot, owner_of, shard_rows, *after)


def event_kernel(plan, n_in, n_after, *refs):
    ins, outs = refs[:n_in], refs[n_in + n_after :]
    for out, parts in zip(outs, plan):
        offset = 0
        for count, sources in parts:

            @pl.loop(0, count, unroll=max(d for d in range(1, 12) if count % d == 0))
            def _(i, out=out, offset=offset, sources=sources):
                total = [ins[ref][start + i].astype(jnp.float32) for ref, start in sources]
                out[offset + i] = sum(total[1:], total[0]).astype(out.dtype)

            offset += count


def event(arrays, plan, after):
    piece = arrays[0].shape[1:]
    vmem = pl.BlockSpec(memory_space=pltpu.VMEM)
    counts = [sum(n for n, _ in parts) for parts in plan]
    return pl.pallas_call(
        functools.partial(event_kernel, plan, len(arrays), len(after)),
        out_shape=[jax.ShapeDtypeStruct((n,) + piece, arrays[0].dtype) for n in counts],
        in_specs=[vmem] * len(arrays) + [pl.BlockSpec(memory_space=pl.ANY)] * len(after),
        out_specs=[vmem] * len(counts),
        compiler_params=pltpu.CompilerParams(vmem_limit_bytes=16 * MIB),
        cost_estimate=pl.CostEstimate(flops=0, bytes_accessed=1024, transcendentals=0),
    )(*arrays, *after)


def times(a, b):
    return jnp.dot(
        a.astype(jnp.bfloat16), b.astype(jnp.bfloat16), preferred_element_type=jnp.float32
    )


def next_iterate(m):
    d = (times(m, m) - 10.0 * m) * (1.0 / 16.0)
    e = times(d, d) + 3.125 * d
    return (625.0 / 256.0) * m + times(e, m)


def root_of(stat):
    c = jnp.sqrt(jnp.sum(stat * stat))
    m0 = stat / c
    m1 = next_iterate(m0)
    m2 = next_iterate(m1)
    t = times(m0, m1)
    pair = m0 + m1
    total = times(5.0 * pair - t, m2) + 5.0 * t - 25.0 * (pair + m2)
    n = stat.shape[0]
    on_diagonal = lax.broadcasted_iota(jnp.int32, (n, n), 0) == lax.broadcasted_iota(
        jnp.int32, (n, n), 1
    )
    total = total + jnp.where(on_diagonal, 125.0, 0.0)
    return total * (lax.rsqrt(jnp.sqrt(c)) * (1.0 / 64.0))


def roots_kernel(owner_ref, refresh_ref, slot_ref, ls_ref, rs_ref, lr_ref, rr_ref, _, left_ref, right_ref, token_ref):
    token_ref[...] = jnp.zeros_like(token_ref)
    slot = slot_ref[0]

    def look(i, found):
        return found | jnp.where(owner_ref[refresh_ref[i]] == slot, 1, 0)

    fresh = lax.fori_loop(0, refresh_ref.shape[0], look, jnp.int32(0))

    @pl.when(fresh == 1)
    def _():
        left_ref[...] = root_of(ls_ref[...])
        right_ref[...] = root_of(rs_ref[...])

    @pl.when(fresh == 0)
    def _():
        left_ref[...] = lr_ref[...]
        right_ref[...] = rr_ref[...]


def roots(owner_of, refresh, slot, stats_and_roots, after):
    vmem = pl.BlockSpec(memory_space=pltpu.VMEM)
    smem = pl.BlockSpec(memory_space=pltpu.SMEM)
    stat = stats_and_roots[0]
    return pl.pallas_call(
        roots_kernel,
        out_shape=[jax.ShapeDtypeStruct(stat.shape, stat.dtype)] * 2
        + [jax.ShapeDtypeStruct((8, 128), jnp.float32)],
        in_specs=[smem] * 3 + [vmem] * 4 + [pl.BlockSpec(memory_space=pl.ANY)],
        out_specs=[vmem] * 3,
        compiler_params=pltpu.CompilerParams(vmem_limit_bytes=32 * MIB),
        cost_estimate=pl.CostEstimate(flops=0, bytes_accessed=1024, transcendentals=0),
    )(owner_of, refresh, slot, *stats_and_roots, after)


def finish_kernel(grad_ref, ls_ref, rs_ref, lr_ref, rr_ref, up_out, nl_out, nr_out, up_ref, nl_ref, nr_ref, sems):
    writes = [
        pltpu.make_async_copy(src, dst, sems.at[k])
        for k, (src, dst) in enumerate(((up_ref, up_out), (nl_ref, nl_out), (nr_ref, nr_out)))
    ]
    grad = grad_ref[...]
    coeff = SHARE / grad.shape[1]
    f32 = jnp.float32
    gram = lax.dot_general(grad, grad, (((1,), (1,)), ((), ())), preferred_element_type=f32)
    nl_ref[...] = DECAY * ls_ref[...] + coeff * gram
    writes[1].start()
    gram = lax.dot_general(grad, grad, (((0,), (0,)), ((), ())), preferred_element_type=f32)
    nr_ref[...] = DECAY * rs_ref[...] + coeff * gram
    writes[2].start()
    left_part = jnp.dot(lr_ref[...].astype(jnp.bfloat16), grad, preferred_element_type=f32)
    up_ref[...] = jnp.dot(
        left_part.astype(jnp.bfloat16),
        rr_ref[...].astype(jnp.bfloat16),
        preferred_element_type=f32,
    ).astype(jnp.bfloat16)
    writes[0].start()
    for write in writes:
        write.wait()


def finish(grad, left_stat, right_stat, left_root, right_root):
    vmem = pl.BlockSpec(memory_space=pltpu.VMEM)
    out_shape = [
        jax.ShapeDtypeStruct(grad.shape, jnp.bfloat16),
        jax.ShapeDtypeStruct(left_stat.shape, jnp.float32),
        jax.ShapeDtypeStruct(right_stat.shape, jnp.float32),
    ]
    return pl.pallas_call(
        finish_kernel,
        out_shape=out_shape,
        in_specs=[vmem] * 5,
        out_specs=[pl.BlockSpec(memory_space=pl.ANY)] * 3,
        scratch_shapes=[pltpu.VMEM(x.shape, x.dtype) for x in out_shape]
        + [pltpu.SemaphoreType.DMA((3,))],
        compiler_params=pltpu.CompilerParams(vmem_limit_bytes=16 * MIB),
        cost_estimate=pl.CostEstimate(flops=4 * 2 * 512**3, bytes_accessed=7 * MIB, transcendentals=0),
    )(grad, left_stat, right_stat, left_root, right_root)


def per_device(grad_parts, owner_of, refresh, left_stat, right_stat, left_root, right_root):
    n_owner = lax.axis_size("owner")
    n_slots = lax.axis_size("dp") * n_owner
    slot = (lax.axis_index("dp") * n_owner + lax.axis_index("owner")).reshape(1)
    shard_rows = grad_parts[0]
    streams = build_streams(n_owner)
    def step(stream, number, x):
        return lax.ppermute(x, AXES, route(n_slots, n_owner, stream[2], number))

    def groups(first):
        return [stream + (first,) for stream in streams]

    def steps(number, sent):
        return [step(stream, number, x) for stream, x in zip(streams, sent)]

    def add(number, got, kept, token):
        arrays = [x for pair in zip(got, kept) for x in pair]
        halves = [count * (2 if number == 1 else 1) for _, count, _ in streams]

        def part(second):
            return [
                [(half, [(2 * k, second * half), (2 * k + 1, second * half)])]
                for k, half in enumerate(halves)
            ]

        sent = event(arrays, part(1), (token,))
        kept = event(arrays, part(0), (sent[0],))
        return sent, kept, kept[0]

    def total(got, kept, token):
        arrays = [x for pair in zip(got, kept) for x in pair]
        parts = [(count, [(2 * k, 0), (2 * k + 1, 0)]) for k, (_, count, _) in enumerate(streams)]
        return event(arrays, [parts], (token,))[0]

    def to_owners(x):
        x = lax.all_to_all(x, "owner", split_axis=0, concat_axis=0, tiled=True)
        return x.reshape(-1, x.shape[2])

    *sent, token = pick(slot, n_owner, owner_of, shard_rows, groups(1), chunks=CHUNKS)
    got = steps(0, sent)
    *kept, token = pick(slot, n_owner, owner_of, shard_rows, groups(0), (token,))
    stats_and_roots = [x[0] for x in (left_stat, right_stat, left_root, right_root)]
    new_left_root, new_right_root, token = roots(
        owner_of, refresh, slot, stats_and_roots, token
    )
    for number in (1, 2):
        sent, kept, token = add(number, got, kept, token)
        got = steps(number, sent)
    grad = total(got, kept, token)
    update, new_left, new_right = finish(to_owners(grad), *stats_and_roots)
    return (
        update[None],
        new_left[None],
        new_right[None],
        new_left_root[None],
        new_right_root[None],
    )


def solution(mesh):
    owned = P(AXES, None, None)
    return jax.shard_map(
        per_device,
        mesh=mesh,
        in_specs=(P("dp", None, "owner", None), P(), P(), owned, owned, owned, owned),
        out_specs=(owned,) * 5,
        check_vma=False,
    )
```

time: 83.2 us -> 76.6 us (0.921); the launches traced: 81.6 us -> 76.2 us
  blocking collectives: 0 us -> 29.3 us
  waiting for transfers between devices: 37.5 us -> 24.4 us
  starting transfers between devices: 18.2 us -> 7.2 us
  Pallas kernels: 15.8 us -> 10.7 us
  local copies, waits for them, and re-layouts: 7.26 us -> 3.83 us
  other arithmetic: 2.11 us -> 0 us
    all_to_all x0 -> x1, blocking collectives: none -> 29.3 us  [to_owners(): x = lax.all_to_all(x, 'owner', split_axis=0, concat_axis=0, tiled=True)]
    all_to_all x1 -> x0, starting transfers between devices: 11.5 us -> none  [per_device(): lax.all_to_all(outgoing, 'owner', split_axis=0, concat_axis=0, tiled=True)]
    all_to_all x1 -> x0, waiting for transfers between devices: 6.77 us -> none  [per_device(): lax.all_to_all(outgoing, 'owner', split_axis=0, concat_axis=0, tiled=True)]
    ppermute x6, waiting for transfers between devices: 30.7 us -> 24.4 us  [step(): return lax.ppermute(x, AXES, route(n_slots, n_owner, stream[2], number))]
    pallas_call x5 -> x9, Pallas kernels: 15.8 us -> 10.7 us  [the longest x2 4.93 us: pick(): pl.pallas_call(functools.partial(pick_kernel, groups, n_owner, chunks, le...]
    unnamed x22 -> x16, local copies, waits for them, and re-layouts: 6.56 us -> 3.83 us
    convert_element_type x6 -> x0, other arithmetic: 1.27 us -> none  [plus(): return (a.astype(jnp.float32) + b.astype(jnp.float32)).astype(jnp.bfloat16)]
    concatenate x1 -> x0, other arithmetic: 0.84 us -> none  [per_device(): outgoing = jnp.concatenate(summed, axis=0)]
  transfers between devices with their start and end apart: 7 -> 6, of which waited for: 5 -> 6; matrix products, arithmetic and copies ran while one was open for 1% -> 0% of each run, Pallas kernels for 14% -> 5%
where the time goes in v3:
time: 76.6 us; the launch traced here: 76.2 us
  blocking collectives  29.3 us (38%)
  waiting for transfers between devices  24.4 us (32%)
  Pallas kernels  10.7 us (14%)
  starting transfers between devices  7.2 us (9%)
  local copies, waits for them, and re-layouts  3.83 us (5%)
    all_to_all x1, blocking collectives, to_owners(): x = lax.all_to_all(x, 'owner', split_axis=0, concat_axis=0, tiled=True)  29.3 us
    ppermute x6, waiting for transfers between devices, step(): return lax.ppermute(x, AXES, route(n_slots, n_owner, stream[2], number))  24.4 us
    ppermute x6, starting transfers between devices, step(): return lax.ppermute(x, AXES, route(n_slots, n_owner, stream[2], number))  7.2 us
    pallas_call x2, Pallas kernels, pick(): pl.pallas_call(functools.partial(pick_kernel, groups, n_owner, chunks, le...  4.93 us
    unnamed x16, local copies, waits for them, and re-layouts  3.83 us
    pallas_call x1, Pallas kernels, finish(): pl.pallas_call(finish_kernel, out_shape=out_shape, in_specs=[vmem] * 5, o...  2.56 us
    pallas_call x1, Pallas kernels, roots(): pl.pallas_call(roots_kernel, out_shape=[jax.ShapeDtypeStruct(stat.shape,...  2.33 us
  transfers between devices with their start and end apart: 6, of which 6 were waited for; matrix products, arithmetic and copies ran while one was open for 0% of the time, Pallas kernels for 5%

profile of v3, /device:TPU:6, one launch (start us, length us, event | category | flops | bytes accessed | tf_op | source)
XLA Modules:
  0.0 76.2 jit_solution(15114274707806950527)
XLA Ops:
  0.6 0.0 copy-start.5
  0.6 3.7 %shard_map.110 = (bf16[88,16,512]{2,1,0:T(8,128)(2,1)}, bf16[40,16,512]{2,1,0:T(8,128)(2,1)}, f32[8,128]{1,0:T(8,128)}) custom-call(s32[1]{0:T(128)} %bitcast.slot_ref, s32[256]{0:T(256)} %owner_ref.5, bf16[256,16,512]{2,1,0:T(8,128)(2,1)} %bitcast.12), custom_call_target="tpu_custom_call" | custom-call | bytes 1024 | tf_op jit(solution)/shard_map/pallas_call | solution.py:99
  4.4 0.9 %collective-permute-start = (bf16[88,16,512]{2,1,0:T(8,128)(2,1)}, bf16[88,16,512]{2,1,0:T(8,128)(2,1)S(1)}, u32[]{:S(2)}, u32[]{:S(2)}) collective-permute-start(bf16[88,16,512]{2,1,0:T(8,128)(2,1)} %get-tuple-element.25), channel_id=1, source_target_pairs={{0,64},{1,193},{2,66},{3,195},{4,68},{5,197},{6,70},{7,199},{8,72}... | collective-permute-start | bytes 4325384 | tf_op jit(solution)/shard_map/ppermute | solution.py:256
  5.3 1.6 %collective-permute-start.1 = (bf16[40,16,512]{2,1,0:T(8,128)(2,1)}, bf16[40,16,512]{2,1,0:T(8,128)(2,1)S(1)}, u32[]{:S(2)}, u32[]{:S(2)}) collective-permute-start(bf16[40,16,512]{2,1,0:T(8,128)(2,1)} %get-tuple-element.28), channel_id=1, source_target_pairs={{0,32},{1,33},{2,34},{3,35},{4,36},{5,37},{6,38},{7,39},{8,40},{9,... | collective-permute-start | bytes 1966088 | tf_op jit(solution)/shard_map/ppermute | solution.py:256
  6.9 0.0 copy-done.5
  6.9 2.2 %copy-done = bf16[1,256,16,512]{3,2,1,0:T(8,128)(2,1)S(1)} copy-done((bf16[1,256,16,512]{3,2,1,0:T(8,128)(2,1)S(1)}, bf16[1,256,16,512]{3,2,1,0:T(8,128)(2,1)}, u32[]{:S(2)}) %copy-start) | copy-done | bytes 4194328
  9.1 0.7 copy-done.6
  9.8 0.0 copy-start.7
  9.8 1.2 %shard_map.111 = (bf16[88,16,512]{2,1,0:T(8,128)(2,1)S(1)}, bf16[40,16,512]{2,1,0:T(8,128)(2,1)S(1)}, f32[8,128]{1,0:T(8,128)S(1)}) custom-call(s32[1]{0:T(128)} %bitcast.slot_ref, s32[256]{0:T(256)S(1)} %copy-done.5, bf16[256,16,512]{2,1,0:T(8,128)(2,1)S(1)} %bitcast.13, f32[8,128]{1,0:T(8,128)S(1)} %copy-done.6), custom_call_target="tpu_custom_call" | custom-call | bytes 1024 | tf_op jit(solution)/shard_map/pallas_call | solution.py:99
  11.0 0.0 copy-done.1
  11.0 0.3 copy-done.2
  11.3 0.3 copy-done.3
  11.6 0.3 copy-done.4
  11.9 0.0 copy-done.7
  11.9 2.3 %shard_map.112 = (f32[512,512]{1,0:T(8,128)}, f32[512,512]{1,0:T(8,128)}, f32[8,128]{1,0:T(8,128)S(1)}) custom-call(s32[256]{0:T(256)S(1)} %copy-done.5, s32[32]{0:T(128)S(1)} %copy-done.7, s32[1]{0:T(128)} %bitcast.slot_ref, f32[512,512]{1,0:T(8,128)S(1)} %bitcast.14, f32[512,512]{1,0:T(8,128)S(1)} %bitcast.16, f32[512,512]{1,0:T(8,128)S(1)} %bitcast.18, ...), custom_call_target="tpu_custom_call" | custom-call | bytes 1024 | tf_op jit(solution)/shard_map/pallas_call | solution.py:194
  14.3 7.0 %collective-permute-done.1.refs_2_ = bf16[40,16,512]{2,1,0:T(8,128)(2,1)S(1)} collective-permute-done((bf16[40,16,512]{2,1,0:T(8,128)(2,1)}, bf16[40,16,512]{2,1,0:T(8,128)(2,1)S(1)}, u32[]{:S(2)}, u32[]{:S(2)}) %collective-permute-start.1) | collective-permute-done | bytes 655392 | tf_op jit(solution)/shard_map/ppermute | solution.py:256
  21.3 2.4 %collective-permute-done.refs_0_ = bf16[88,16,512]{2,1,0:T(8,128)(2,1)S(1)} collective-permute-done((bf16[88,16,512]{2,1,0:T(8,128)(2,1)}, bf16[88,16,512]{2,1,0:T(8,128)(2,1)S(1)}, u32[]{:S(2)}, u32[]{:S(2)}) %collective-permute-start) | collective-permute-done | bytes 1441824 | tf_op jit(solution)/shard_map/ppermute | solution.py:256
  23.7 0.3 shard_map.113
  24.0 1.7 %collective-permute-start.2 = (bf16[44,16,512]{2,1,0:T(8,128)(2,1)S(1)}, bf16[44,16,512]{2,1,0:T(8,128)(2,1)S(1)}, u32[]{:S(2)}, u32[]{:S(2)}) collective-permute-start(bf16[44,16,512]{2,1,0:T(8,128)(2,1)S(1)} %get-tuple-element.32.refs_4_), channel_id=1, source_target_pairs={{0,32},{1,65},{2,34},{3,67},{4,36},{5,69},{6,38},{7,71},{8,40},{9,... | collective-permute-start | bytes 2162696 | tf_op jit(solution)/shard_map/ppermute | solution.py:256
  25.6 0.7 collective-permute-start.3
  26.4 0.3 shard_map.114
  26.6 8.2 %collective-permute-done.3.refs_2_ = bf16[20,16,512]{2,1,0:T(8,128)(2,1)S(1)} collective-permute-done((bf16[20,16,512]{2,1,0:T(8,128)(2,1)S(1)}, bf16[20,16,512]{2,1,0:T(8,128)(2,1)S(1)}, u32[]{:S(2)}, u32[]{:S(2)}) %collective-permute-start.3) | collective-permute-done | bytes 327712 | tf_op jit(solution)/shard_map/ppermute | solution.py:256
  34.9 0.5 collective-permute-done.2.refs_0_
  35.3 0.1 shard_map.115
  35.5 2.3 %collective-permute-start.4 = (bf16[22,16,512]{2,1,0:T(8,128)(2,1)S(1)}, bf16[22,16,512]{2,1,0:T(8,128)(2,1)S(1)}, u32[]{:S(2)}, u32[]{:S(2)}) collective-permute-start(bf16[22,16,512]{2,1,0:T(8,128)(2,1)S(1)} %get-tuple-element.36.refs_4_), channel_id=1, source_target_pairs={{0,192},{1,33},{2,194},{3,35},{4,196},{5,37},{6,198},{7,39},{8,200... | collective-permute-start | bytes 1081352 | tf_op jit(solution)/shard_map/ppermute | solution.py:256
  37.8 0.0 collective-permute-start.5
  37.8 0.1 shard_map.116
  37.9 5.2 %collective-permute-done.5.refs_2_ = bf16[10,16,512]{2,1,0:T(8,128)(2,1)S(1)} collective-permute-done((bf16[10,16,512]{2,1,0:T(8,128)(2,1)S(1)}, bf16[10,16,512]{2,1,0:T(8,128)(2,1)S(1)}, u32[]{:S(2)}, u32[]{:S(2)}) %collective-permute-start.5) | collective-permute-done | bytes 163872 | tf_op jit(solution)/shard_map/ppermute | solution.py:256
  43.1 1.1 %collective-permute-done.4.refs_0_ = bf16[22,16,512]{2,1,0:T(8,128)(2,1)S(1)} collective-permute-done((bf16[22,16,512]{2,1,0:T(8,128)(2,1)S(1)}, bf16[22,16,512]{2,1,0:T(8,128)(2,1)S(1)}, u32[]{:S(2)}, u32[]{:S(2)}) %collective-permute-start.4) | collective-permute-done | bytes 360480 | tf_op jit(solution)/shard_map/ppermute | solution.py:256
  44.2 0.1 shard_map.117
  44.3 29.3 %all_to_all.5 = bf16[32,16,512]{2,1,0:T(8,128)(2,1)S(1)} all-to-all(bf16[32,16,512]{2,1,0:T(8,128)(2,1)S(1)} %shard_map.117), channel_id=1, replica_groups=mesh['dp'=8,'owner'=32] {'owner'}, dimensions={0} | all-to-all | bytes 1048576 | tf_op jit(solution)/shard_map/all_to_all | solution.py:284
  73.6 2.6 %shard_map.118 = (bf16[512,512]{1,0:T(8,128)(2,1)}, f32[512,512]{1,0:T(8,128)}, f32[512,512]{1,0:T(8,128)}) custom-call(bf16[512,512]{1,0:T(8,128)(2,1)S(1)} %bitcast.22, f32[512,512]{1,0:T(8,128)S(1)} %bitcast.15, f32[512,512]{1,0:T(8,128)S(1)} %bitcast.17, f32[512,512]{1,0:T(8,128)S(1)} %bitcast.19, f32[512,512]{1,0:T(8,128)S(1)} %bitcast.21), custom_call_target="tpu_custom_call" | custom-call | flops 1073741824 | bytes 7340032 | tf_op jit(solution)/shard_map/pallas_call | solution.py:237
  (6 shorter events, 0.0 us)
Async XLA Ops:
  0.6 6.2 %copy-start.5 = (s32[256]{0:T(256)S(1)}, s32[256]{0:T(256)}, u32[]{:S(2)}) copy-start(s32[256]{0:T(256)} %owner_ref.5) | copy-start | bytes 3076
  4.4 19.3 %collective-permute-start = (bf16[88,16,512]{2,1,0:T(8,128)(2,1)}, bf16[88,16,512]{2,1,0:T(8,128)(2,1)S(1)}, u32[]{:S(2)}, u32[]{:S(2)}) collective-permute-start(bf16[88,16,512]{2,1,0:T(8,128)(2,1)} %get-tuple-element.25), channel_id=1, source_target_pairs={{0,64},{1,193},{2,66},{3,195},{4,68},{5,197},{6,70},{7,199},{8,72}... | collective-permute-start | bytes 4325384 | tf_op jit(solution)/shard_map/ppermute | solution.py:256
  5.3 16.0 %collective-permute-start.1 = (bf16[40,16,512]{2,1,0:T(8,128)(2,1)}, bf16[40,16,512]{2,1,0:T(8,128)(2,1)S(1)}, u32[]{:S(2)}, u32[]{:S(2)}) collective-permute-start(bf16[40,16,512]{2,1,0:T(8,128)(2,1)} %get-tuple-element.28), channel_id=1, source_target_pairs={{0,32},{1,33},{2,34},{3,35},{4,36},{5,37},{6,38},{7,39},{8,40},{9,... | collective-permute-start | bytes 1966088 | tf_op jit(solution)/shard_map/ppermute | solution.py:256
  6.9 2.2 %copy-start = (bf16[1,256,16,512]{3,2,1,0:T(8,128)(2,1)S(1)}, bf16[1,256,16,512]{3,2,1,0:T(8,128)(2,1)}, u32[]{:S(2)}) copy-start(bf16[1,256,16,512]{3,2,1,0:T(8,128)(2,1)} %param.7) | copy-start | bytes 12582916
  9.1 0.7 copy-start.6
  9.8 1.2 %copy-start.1 = (f32[1,512,512]{2,1,0:T(8,128)S(1)}, f32[1,512,512]{2,1,0:T(8,128)}, u32[]{:S(2)}) copy-start(f32[1,512,512]{2,1,0:T(8,128)} %param.10) | copy-start | bytes 3145732
  9.8 1.5 %copy-start.2 = (f32[1,512,512]{2,1,0:T(8,128)S(1)}, f32[1,512,512]{2,1,0:T(8,128)}, u32[]{:S(2)}) copy-start(f32[1,512,512]{2,1,0:T(8,128)} %param.11) | copy-start | bytes 3145732
  9.8 1.9 %copy-start.3 = (f32[1,512,512]{2,1,0:T(8,128)S(1)}, f32[1,512,512]{2,1,0:T(8,128)}, u32[]{:S(2)}) copy-start(f32[1,512,512]{2,1,0:T(8,128)} %param.12) | copy-start | bytes 3145732
  9.8 2.2 %copy-start.4 = (f32[1,512,512]{2,1,0:T(8,128)S(1)}, f32[1,512,512]{2,1,0:T(8,128)}, u32[]{:S(2)}) copy-start(f32[1,512,512]{2,1,0:T(8,128)} %param.13) | copy-start | bytes 3145732
  9.8 2.2 %copy-start.7 = (s32[32]{0:T(128)S(1)}, s32[32]{0:T(128)}, u32[]{:S(2)}) copy-start(s32[32]{0:T(128)} %refresh_ref.1) | copy-start | bytes 388
  24.0 11.4 %collective-permute-start.2 = (bf16[44,16,512]{2,1,0:T(8,128)(2,1)S(1)}, bf16[44,16,512]{2,1,0:T(8,128)(2,1)S(1)}, u32[]{:S(2)}, u32[]{:S(2)}) collective-permute-start(bf16[44,16,512]{2,1,0:T(8,128)(2,1)S(1)} %get-tuple-element.32.refs_4_), channel_id=1, source_target_pairs={{0,32},{1,65},{2,34},{3,67},{4,36},{5,69},{6,38},{7,71},{8,40},{9,... | collective-permute-start | bytes 2162696 | tf_op jit(solution)/shard_map/ppermute | solution.py:256
  25.6 9.2 %collective-permute-start.3 = (bf16[20,16,512]{2,1,0:T(8,128)(2,1)S(1)}, bf16[20,16,512]{2,1,0:T(8,128)(2,1)S(1)}, u32[]{:S(2)}, u32[]{:S(2)}) collective-permute-start(bf16[20,16,512]{2,1,0:T(8,128)(2,1)S(1)} %get-tuple-element.34), channel_id=1, source_target_pairs={{0,192},{1,193},{2,194},{3,195},{4,196},{5,197},{6,198},{7,199},{8... | collective-permute-start | bytes 983048 | tf_op jit(solution)/shard_map/ppermute | solution.py:256
  35.5 8.7 %collective-permute-start.4 = (bf16[22,16,512]{2,1,0:T(8,128)(2,1)S(1)}, bf16[22,16,512]{2,1,0:T(8,128)(2,1)S(1)}, u32[]{:S(2)}, u32[]{:S(2)}) collective-permute-start(bf16[22,16,512]{2,1,0:T(8,128)(2,1)S(1)} %get-tuple-element.36.refs_4_), channel_id=1, source_target_pairs={{0,192},{1,33},{2,194},{3,35},{4,196},{5,37},{6,198},{7,39},{8,200... | collective-permute-start | bytes 1081352 | tf_op jit(solution)/shard_map/ppermute | solution.py:256
  37.8 5.3 %collective-permute-start.5 = (bf16[10,16,512]{2,1,0:T(8,128)(2,1)S(1)}, bf16[10,16,512]{2,1,0:T(8,128)(2,1)S(1)}, u32[]{:S(2)}, u32[]{:S(2)}) collective-permute-start(bf16[10,16,512]{2,1,0:T(8,128)(2,1)S(1)} %get-tuple-element.38), channel_id=1, source_target_pairs={{0,64},{1,65},{2,66},{3,67},{4,68},{5,69},{6,70},{7,71},{8,72},{9,... | collective-permute-start | bytes 491528 | tf_op jit(solution)/shard_map/ppermute | solution.py:256

commit v4 on v3

--- a/solution.py
+++ b/solution.py
@@ -19,24 +19,25 @@
 X_OF, Y_OF = {"a": 1, "b": 3, "y": 0}, {"a": 0, "b": 0, "y": 1}
 
 
-def build_streams(n_owner):
-    cut = -(-2 * n_owner // 3)
-    return [(0, cut, WIDE), (cut, n_owner - cut, SLIM)]
-
-
-def route(n_slots, n_owner, orders, step):
+def build_streams(n_places):
+    cut = -(-2 * n_places // 3)
+    return [(0, cut, WIDE), (cut, n_places - cut, SLIM)]
+
+
+def route(n_slots, n_owner, orders, step, other=0):
     pairs = []
     for s in range(n_slots):
         data, owner = divmod(s, n_owner)
-        dim = orders[owner % 2][step]
-        to = (data // 2 ^ X_OF[dim]) * 2 + (data % 2 ^ Y_OF[dim])
-        pairs.append((s, to * n_owner + owner))
+        if orders is not None:
+            dim = orders[owner % 2 ^ other][step]
+            data = (data // 2 ^ X_OF[dim]) * 2 + (data % 2 ^ Y_OF[dim])
+        pairs.append((s, data * n_owner + (owner ^ other)))
     return pairs
 
 
-def pick_kernel(groups, n_owner, chunks, n_after, slot_ref, owner_ref, shard_ref, *refs):
-    outs, token = refs[n_after : n_after + len(groups)], refs[n_after + len(groups)]
-    block_at, owners, sem = refs[n_after + len(groups) + 1 :][:3]
+def pick_kernel(plan, n_owner, chunks, n_after, slot_ref, owner_ref, shard_ref, *refs):
+    outs, token = refs[n_after : n_after + len(plan)], refs[n_after + len(plan)]
+    block_at, owners, sem = refs[n_after + len(plan) + 1 :][:3]
     copies = []
     if chunks:
         held, sems = refs[-2:]
@@ -52,7 +53,7 @@
         copy.start()
     token[...] = jnp.zeros_like(token)
     slot = slot_ref[0]
-    data, core = slot // n_owner, lax.rem(slot, 2)
+    data, my_core = slot // n_owner, lax.rem(slot, 2)
     x, y_lo = data // 2, lax.rem(data, 2)
     read_owners.wait()
 
@@ -62,26 +63,29 @@
 
     for copy in copies:
         copy.wait()
-    for out, (begin, count, orders, first) in zip(outs, groups):
-        for second in (0, 1):
-            for third in (0, 1):
-                bits = (first, second, third)
-                on_x, on_y = [0, 0], [0, 0]
-                for c in (0, 1):
-                    for dim, bit in zip(orders[c], (first, second, third)):
-                        on_x[c] ^= X_OF[dim] * bit
-                        on_y[c] ^= Y_OF[dim] * bit
-                to_x = x ^ jnp.where(core == 0, on_x[0], on_x[1])
-                to_y = y_lo ^ jnp.where(core == 0, on_y[0], on_y[1])
-                base = (to_x * 2 + to_y) * n_owner + begin
-                offset = (2 * second + third) * count
-
-                @pl.loop(0, count, unroll=max(d for d in range(1, 12) if count % d == 0))
-                def _(i, out=out, offset=offset, base=base):
-                    out[offset + i] = held[block_at[base + i]]
-
-
-def pick(slot, n_owner, owner_of, shard_rows, groups, after=(), chunks=0):
+    for out, groups in zip(outs, plan):
+        offset = 0
+        for begin, count, orders, first, other in groups:
+            core = 1 - my_core if other else my_core
+            for second in (0, 1):
+                for third in (0, 1):
+                    on_x, on_y = [0, 0], [0, 0]
+                    for c in (0, 1):
+                        for dim, bit in zip(orders[c], (first, second, third)):
+                            on_x[c] ^= X_OF[dim] * bit
+                            on_y[c] ^= Y_OF[dim] * bit
+                    to_x = x ^ jnp.where(core == 0, on_x[0], on_x[1])
+                    to_y = y_lo ^ jnp.where(core == 0, on_y[0], on_y[1])
+                    base = (to_x * 2 + to_y) * n_owner + 2 * begin + core
+
+                    @pl.loop(0, count, unroll=count)
+                    def _(i, out=out, offset=offset, base=base):
+                        out[offset + i] = held[block_at[base + 2 * i]]
+
+                    offset += count
+
+
+def pick(slot, n_owner, owner_of, shard_rows, plan, after=(), chunks=0):
     _, rows, width = shard_rows.shape
     vmem = pl.BlockSpec(memory_space=pltpu.VMEM)
     smem = pl.BlockSpec(memory_space=pltpu.SMEM)
@@ -97,18 +101,53 @@
             pltpu.SemaphoreType.DMA((chunks,)),
         ]
     return pl.pallas_call(
-        functools.partial(pick_kernel, groups, n_owner, chunks, len(after)),
+        functools.partial(pick_kernel, plan, n_owner, chunks, len(after)),
         out_shape=[
-            jax.ShapeDtypeStruct((4 * count, rows, width), shard_rows.dtype)
-            for _, count, _, _ in groups
+            jax.ShapeDtypeStruct((4 * sum(g[1] for g in groups), rows, width), shard_rows.dtype)
+            for groups in plan
         ]
         + [jax.ShapeDtypeStruct((8, 128), jnp.float32)],
         in_specs=[smem, anywhere, anywhere if chunks else vmem] + [anywhere] * len(after),
-        out_specs=[vmem] * (len(groups) + 1),
+        out_specs=[vmem] * (len(plan) + 1),
         scratch_shapes=scratch,
         compiler_params=pltpu.CompilerParams(vmem_limit_bytes=(MOST_MIB if chunks else 16) * MIB),
         cost_estimate=pl.CostEstimate(flops=0, bytes_accessed=1024, transcendentals=0),
     )(slot, owner_of, shard_rows, *after)
+
+
+def first_sum_kernel(counts, second, slot_ref, handed_ref, *refs):
+    n = len(counts)
+    core = lax.rem(slot_ref[0], 2)
+    offset = 0
+    for k, count in enumerate(counts):
+        same, other, own, out = refs[3 * k], refs[3 * k + 1], refs[3 * k + 2], refs[3 * n + 1 + k]
+
+        @pl.loop(0, 2 * count, unroll=count)
+        def _(i, same=same, other=other, own=own, out=out, offset=offset, count=count):
+            j = 2 * count * second + i
+            f32 = jnp.float32
+            out[2 * i + core] = (same[j].astype(f32) + own[j].astype(f32)).astype(out.dtype)
+            out[2 * i + 1 - core] = (
+                other[j].astype(f32) + handed_ref[offset + j].astype(f32)
+            ).astype(out.dtype)
+
+        offset += 4 * count
+
+
+def first_sum(slot, counts, second, handed, arrays, after):
+    vmem = pl.BlockSpec(memory_space=pltpu.VMEM)
+    return pl.pallas_call(
+        functools.partial(first_sum_kernel, counts, second),
+        out_shape=[
+            jax.ShapeDtypeStruct((4 * count,) + handed.shape[1:], handed.dtype) for count in counts
+        ],
+        in_specs=[pl.BlockSpec(memory_space=pltpu.SMEM)]
+        + [vmem] * (1 + len(arrays))
+        + [pl.BlockSpec(memory_space=pl.ANY)],
+        out_specs=[vmem] * len(counts),
+        compiler_params=pltpu.CompilerParams(vmem_limit_bytes=16 * MIB),
+        cost_estimate=pl.CostEstimate(flops=0, bytes_accessed=1024, transcendentals=0),
+    )(slot, handed, *arrays, after)
 
 
 def event_kernel(plan, n_in, n_after, *refs):
@@ -251,49 +290,56 @@
     n_slots = lax.axis_size("dp") * n_owner
     slot = (lax.axis_index("dp") * n_owner + lax.axis_index("owner")).reshape(1)
     shard_rows = grad_parts[0]
-    streams = build_streams(n_owner)
-    def step(stream, number, x):
-        return lax.ppermute(x, AXES, route(n_slots, n_owner, stream[2], number))
-
-    def groups(first):
-        return [stream + (first,) for stream in streams]
-
-    def steps(number, sent):
-        return [step(stream, number, x) for stream, x in zip(streams, sent)]
-
-    def add(number, got, kept, token):
-        arrays = [x for pair in zip(got, kept) for x in pair]
-        halves = [count * (2 if number == 1 else 1) for _, count, _ in streams]
-
-        def part(second):
-            return [
-                [(half, [(2 * k, second * half), (2 * k + 1, second * half)])]
-                for k, half in enumerate(halves)
-            ]
-
-        sent = event(arrays, part(1), (token,))
-        kept = event(arrays, part(0), (sent[0],))
-        return sent, kept, kept[0]
+    streams = build_streams(n_owner // 2)
+    counts = [2 * count for _, count, _ in streams]
+
+    def send(x, *how):
+        return lax.ppermute(x, AXES, route(n_slots, n_owner, *how))
+
+    def steps(number, sent, other=0):
+        return [send(x, orders, number, other) for (_, _, orders), x in zip(streams, sent)]
 
     def total(got, kept, token):
         arrays = [x for pair in zip(got, kept) for x in pair]
-        parts = [(count, [(2 * k, 0), (2 * k + 1, 0)]) for k, (_, count, _) in enumerate(streams)]
+        parts = [(count, [(2 * k, 0), (2 * k + 1, 0)]) for k, count in enumerate(counts)]
         return event(arrays, [parts], (token,))[0]
 
     def to_owners(x):
-        x = lax.all_to_all(x, "owner", split_axis=0, concat_axis=0, tiled=True)
+        groups = [list(range(core, n_owner, 2)) for core in (0, 1)]
+        x = x.reshape(n_owner // 2, -1, x.shape[2])
+        x = lax.all_to_all(
+            x, "owner", split_axis=0, concat_axis=0, tiled=True, axis_index_groups=groups
+        )
         return x.reshape(-1, x.shape[2])
 
-    *sent, token = pick(slot, n_owner, owner_of, shard_rows, groups(1), chunks=CHUNKS)
-    got = steps(0, sent)
-    *kept, token = pick(slot, n_owner, owner_of, shard_rows, groups(0), (token,))
+    plan = [[stream + (0, 1) for stream in streams]]
+    plan += [[stream + (1, other)] for other in (0, 1) for stream in streams]
+    handed, *sent, token = pick(slot, n_owner, owner_of, shard_rows, plan, chunks=CHUNKS)
+    handed = send(handed, None, 0, 1)
+    same, other = steps(0, sent[: len(streams)]), steps(0, sent[len(streams) :], 1)
+    plan = [[stream + (0, 0)] for stream in streams]
+    *own, token = pick(slot, n_owner, owner_of, shard_rows, plan, (token,))
     stats_and_roots = [x[0] for x in (left_stat, right_stat, left_root, right_root)]
     new_left_root, new_right_root, token = roots(
         owner_of, refresh, slot, stats_and_roots, token
     )
-    for number in (1, 2):
-        sent, kept, token = add(number, got, kept, token)
-        got = steps(number, sent)
+    places = [count for _, count, _ in streams]
+    arrays = [x for three in zip(same, other, own) for x in three]
+    sent = first_sum(slot, places, 1, handed, arrays, token)
+    got = steps(1, sent)
+    kept = first_sum(slot, places, 0, handed, arrays, sent[0])
+
+    def part(second):
+        return [
+            [(count, [(2 * k, second * count), (2 * k + 1, second * count)])]
+            for k, count in enumerate(counts)
+        ]
+
+    arrays = [x for pair in zip(got, kept) for x in pair]
+    sent = event(arrays, part(1), (kept[0],))
+    got = steps(2, sent)
+    kept = event(arrays, part(0), (sent[0],))
+    token = kept[0]
     grad = total(got, kept, token)
     update, new_left, new_right = finish(to_owners(grad), *stats_and_roots)
     return (

time: 76.6 us -> 75.2 us (0.982)
  starting transfers between devices: 7.2 us -> 9.17 us
  blocking collectives: 29.3 us -> 27.4 us
  waiting for transfers between devices: 24.4 us -> 23.3 us
    ppermute x6 -> x9, starting transfers between devices: 7.2 us -> 9.17 us  [send(): return lax.ppermute(x, AXES, route(n_slots, n_owner, *how))]
    all_to_all x1, blocking collectives: 29.3 us -> 27.4 us  [to_owners(): lax.all_to_all(x, 'owner', split_axis=0, concat_axis=0, tiled=True, axis_...]
    ppermute x6 -> x9, waiting for transfers between devices: 24.4 us -> 23.3 us  [send(): return lax.ppermute(x, AXES, route(n_slots, n_owner, *how))]
    pallas_call x2 -> x4, Pallas kernels: 4.93 us -> 5.87 us  [the longest x2 5.32 us: pick(): pl.pallas_call(functools.partial(pick_kernel, plan, n_owner, chunks, len(...]
  transfers between devices with their start and end apart: 6 -> 9, of which waited for: 6 -> 7; matrix products, arithmetic and copies ran while one was open for 0% -> 0% of each run, Pallas kernels for 5% -> 5%
where the time goes in v4:
time: 75.2 us; the launch traced here: 75 us
  blocking collectives  27.4 us (36%)
  waiting for transfers between devices  23.3 us (31%)
  Pallas kernels  11.1 us (15%)
  starting transfers between devices  9.17 us (12%)
  local copies, waits for them, and re-layouts  3.33 us (4%)
    all_to_all x1, blocking collectives, to_owners(): lax.all_to_all(x, 'owner', split_axis=0, concat_axis=0, tiled=True, axis_...  27.4 us
    ppermute x9, waiting for transfers between devices, send(): return lax.ppermute(x, AXES, route(n_slots, n_owner, *how))  23.3 us
    ppermute x9, starting transfers between devices, send(): return lax.ppermute(x, AXES, route(n_slots, n_owner, *how))  9.17 us
    pallas_call x2, Pallas kernels, pick(): pl.pallas_call(functools.partial(pick_kernel, plan, n_owner, chunks, len(...  5.32 us
    unnamed x16, local copies, waits for them, and re-layouts  3.33 us
    pallas_call x1, Pallas kernels, finish(): pl.pallas_call(finish_kernel, out_shape=out_shape, in_specs=[vmem] * 5, o...  2.56 us
    pallas_call x1, Pallas kernels, roots(): pl.pallas_call(roots_kernel, out_shape=[jax.ShapeDtypeStruct(stat.shape,...  2.33 us
  transfers between devices with their start and end apart: 9, of which 7 were waited for; matrix products, arithmetic and copies ran while one was open for 0% of the time, Pallas kernels for 5%

profile of v4, /device:TPU:6, one launch (start us, length us, event | category | flops | bytes accessed | tf_op | source)
XLA Modules:
  0.0 75.0 jit_solution(1286968789052431390)
XLA Ops:
  0.7 4.3 %shard_map.110 = (bf16[64,16,512]{2,1,0:T(8,128)(2,1)}, bf16[44,16,512]{2,1,0:T(8,128)(2,1)}, bf16[20,16,512]{2,1,0:T(8,128)(2,1)}, bf16[44,16,512]{2,1,0:T(8,12...) custom-call(s32[1]{0:T(128)} %bitcast.slot_ref, s32[256]{0:T(256)} %owner_ref.5, bf16[256,16,512]{2,1,0:T(8,128)(2,1)} %bitcast.13), custom_call_target="tpu_custom_call" | custom-call | bytes 1024 | tf_op jit(solution)/shard_map/pallas_call | solution.py:103
  4.9 0.1 collective-permute-start
  5.0 0.9 %collective-permute-start.1 = (bf16[44,16,512]{2,1,0:T(8,128)(2,1)}, bf16[44,16,512]{2,1,0:T(8,128)(2,1)S(1)}, u32[]{:S(2)}, u32[]{:S(2)}) collective-permute-start(bf16[44,16,512]{2,1,0:T(8,128)(2,1)} %get-tuple-element.29), channel_id=1, source_target_pairs={{0,64},{1,193},{2,66},{3,195},{4,68},{5,197},{6,70},{7,199},{8,72}... | collective-permute-start | bytes 2162696 | tf_op jit(solution)/shard_map/ppermute | solution.py:297
  6.0 2.1 %collective-permute-start.2 = (bf16[44,16,512]{2,1,0:T(8,128)(2,1)}, bf16[44,16,512]{2,1,0:T(8,128)(2,1)S(1)}, u32[]{:S(2)}, u32[]{:S(2)}) collective-permute-start(bf16[44,16,512]{2,1,0:T(8,128)(2,1)} %get-tuple-element.30), channel_id=1, source_target_pairs={{0,193},{1,64},{2,195},{3,66},{4,197},{5,68},{6,199},{7,70},{8,201... | collective-permute-start | bytes 2162696 | tf_op jit(solution)/shard_map/ppermute | solution.py:297
  8.1 1.6 %collective-permute-start.3 = (bf16[20,16,512]{2,1,0:T(8,128)(2,1)}, bf16[20,16,512]{2,1,0:T(8,128)(2,1)S(1)}, u32[]{:S(2)}, u32[]{:S(2)}) collective-permute-start(bf16[20,16,512]{2,1,0:T(8,128)(2,1)} %get-tuple-element.33), channel_id=1, source_target_pairs={{0,32},{1,33},{2,34},{3,35},{4,36},{5,37},{6,38},{7,39},{8,40},{9,... | collective-permute-start | bytes 983048 | tf_op jit(solution)/shard_map/ppermute | solution.py:297
  9.7 0.0 collective-permute-start.4
  9.7 2.2 %copy-done = bf16[1,256,16,512]{3,2,1,0:T(8,128)(2,1)S(1)} copy-done((bf16[1,256,16,512]{3,2,1,0:T(8,128)(2,1)S(1)}, bf16[1,256,16,512]{3,2,1,0:T(8,128)(2,1)}, u32[]{:S(2)}) %copy-start) | copy-done | bytes 4194328
  11.9 0.7 copy-done.6
  12.6 1.1 %shard_map.111 = (bf16[44,16,512]{2,1,0:T(8,128)(2,1)S(1)}, bf16[20,16,512]{2,1,0:T(8,128)(2,1)S(1)}, f32[8,128]{1,0:T(8,128)S(1)}) custom-call(s32[1]{0:T(128)} %bitcast.slot_ref, s32[256]{0:T(256)S(1)} %copy-done.5, bf16[256,16,512]{2,1,0:T(8,128)(2,1)S(1)} %bitcast.14, f32[8,128]{1,0:T(8,128)S(1)} %copy-done.6), custom_call_target="tpu_custom_call" | custom-call | bytes 1024 | tf_op jit(solution)/shard_map/pallas_call | solution.py:103
  13.7 0.1 copy-done.3
  13.8 0.3 copy-done.4
  14.1 2.3 %shard_map.112 = (f32[512,512]{1,0:T(8,128)}, f32[512,512]{1,0:T(8,128)}, f32[8,128]{1,0:T(8,128)S(1)}) custom-call(s32[256]{0:T(256)S(1)} %copy-done.5, s32[32]{0:T(128)S(1)} %copy-done.7, s32[1]{0:T(128)} %bitcast.slot_ref, f32[512,512]{1,0:T(8,128)S(1)} %bitcast.15, f32[512,512]{1,0:T(8,128)S(1)} %bitcast.17, f32[512,512]{1,0:T(8,128)S(1)} %bitcast.19, ...), custom_call_target="tpu_custom_call" | custom-call | bytes 1024 | tf_op jit(solution)/shard_map/pallas_call | solution.py:233
  16.4 2.5 %collective-permute-done.3.refs_3_ = bf16[20,16,512]{2,1,0:T(8,128)(2,1)S(1)} collective-permute-done((bf16[20,16,512]{2,1,0:T(8,128)(2,1)}, bf16[20,16,512]{2,1,0:T(8,128)(2,1)S(1)}, u32[]{:S(2)}, u32[]{:S(2)}) %collective-permute-start.3) | collective-permute-done | bytes 327712 | tf_op jit(solution)/shard_map/ppermute | solution.py:297
  19.0 4.4 %collective-permute-done.4.refs_4_ = bf16[20,16,512]{2,1,0:T(8,128)(2,1)S(1)} collective-permute-done((bf16[20,16,512]{2,1,0:T(8,128)(2,1)}, bf16[20,16,512]{2,1,0:T(8,128)(2,1)S(1)}, u32[]{:S(2)}, u32[]{:S(2)}) %collective-permute-start.4) | collective-permute-done | bytes 327712 | tf_op jit(solution)/shard_map/ppermute | solution.py:297
  23.3 0.8 %collective-permute-done.1.refs_0_ = bf16[44,16,512]{2,1,0:T(8,128)(2,1)S(1)} collective-permute-done((bf16[44,16,512]{2,1,0:T(8,128)(2,1)}, bf16[44,16,512]{2,1,0:T(8,128)(2,1)S(1)}, u32[]{:S(2)}, u32[]{:S(2)}) %collective-permute-start.1) | collective-permute-done | bytes 720928 | tf_op jit(solution)/shard_map/ppermute | solution.py:297
  24.1 0.3 collective-permute-done.2.refs_1_
  24.4 0.0 collective-permute-done.handed_ref
  24.4 0.3 shard_map.113
  24.6 1.7 %collective-permute-start.5 = (bf16[44,16,512]{2,1,0:T(8,128)(2,1)S(1)}, bf16[44,16,512]{2,1,0:T(8,128)(2,1)S(1)}, u32[]{:S(2)}, u32[]{:S(2)}) collective-permute-start(bf16[44,16,512]{2,1,0:T(8,128)(2,1)S(1)} %get-tuple-element.38.refs_6_), channel_id=1, source_target_pairs={{0,32},{1,65},{2,34},{3,67},{4,36},{5,69},{6,38},{7,71},{8,40},{9,... | collective-permute-start | bytes 2162696 | tf_op jit(solution)/shard_map/ppermute | solution.py:297
  26.3 0.5 collective-permute-start.6
  26.8 0.3 shard_map.114
  27.1 9.1 %collective-permute-done.6.refs_2_ = bf16[20,16,512]{2,1,0:T(8,128)(2,1)S(1)} collective-permute-done((bf16[20,16,512]{2,1,0:T(8,128)(2,1)S(1)}, bf16[20,16,512]{2,1,0:T(8,128)(2,1)S(1)}, u32[]{:S(2)}, u32[]{:S(2)}) %collective-permute-start.6) | collective-permute-done | bytes 327712 | tf_op jit(solution)/shard_map/ppermute | solution.py:297
  36.1 0.0 collective-permute-done.5.refs_0_
  36.1 0.1 shard_map.115
  36.3 2.3 %collective-permute-start.7 = (bf16[22,16,512]{2,1,0:T(8,128)(2,1)S(1)}, bf16[22,16,512]{2,1,0:T(8,128)(2,1)S(1)}, u32[]{:S(2)}, u32[]{:S(2)}) collective-permute-start(bf16[22,16,512]{2,1,0:T(8,128)(2,1)S(1)} %get-tuple-element.42.refs_4_), channel_id=1, source_target_pairs={{0,192},{1,33},{2,194},{3,35},{4,196},{5,37},{6,198},{7,39},{8,200... | collective-permute-start | bytes 1081352 | tf_op jit(solution)/shard_map/ppermute | solution.py:297
  38.6 0.0 collective-permute-start.8
  38.6 0.1 shard_map.116
  38.7 5.2 %collective-permute-done.8.refs_2_ = bf16[10,16,512]{2,1,0:T(8,128)(2,1)S(1)} collective-permute-done((bf16[10,16,512]{2,1,0:T(8,128)(2,1)S(1)}, bf16[10,16,512]{2,1,0:T(8,128)(2,1)S(1)}, u32[]{:S(2)}, u32[]{:S(2)}) %collective-permute-start.8) | collective-permute-done | bytes 163872 | tf_op jit(solution)/shard_map/ppermute | solution.py:297
  43.9 1.1 %collective-permute-done.7.refs_0_ = bf16[22,16,512]{2,1,0:T(8,128)(2,1)S(1)} collective-permute-done((bf16[22,16,512]{2,1,0:T(8,128)(2,1)S(1)}, bf16[22,16,512]{2,1,0:T(8,128)(2,1)S(1)}, u32[]{:S(2)}, u32[]{:S(2)}) %collective-permute-start.7) | collective-permute-done | bytes 360480 | tf_op jit(solution)/shard_map/ppermute | solution.py:297
  45.0 0.1 shard_map.117
  45.1 27.4 %all_to_all.5 = bf16[16,32,512]{2,1,0:T(8,128)(2,1)S(1)} all-to-all(bf16[16,32,512]{2,1,0:T(8,128)(2,1)S(1)} %bitcast.24), channel_id=1, replica_groups={{0,2,4,6,8,10,12,14,16,18,20,22,24,26,28,30},{1,3,5,7,9,11,13,15,17,19,..., dimensions={0} | all-to-all | bytes 1048576 | tf_op jit(solution)/shard_map/all_to_all | solution.py:310
  72.5 2.6 %shard_map.118 = (bf16[512,512]{1,0:T(8,128)(2,1)}, f32[512,512]{1,0:T(8,128)}, f32[512,512]{1,0:T(8,128)}) custom-call(bf16[512,512]{1,0:T(8,128)(2,1)S(1)} %bitcast.23, f32[512,512]{1,0:T(8,128)S(1)} %bitcast.16, f32[512,512]{1,0:T(8,128)S(1)} %bitcast.18, f32[512,512]{1,0:T(8,128)S(1)} %bitcast.20, f32[512,512]{1,0:T(8,128)S(1)} %bitcast.22), custom_call_target="tpu_custom_call" | custom-call | flops 1073741824 | bytes 7340032 | tf_op jit(solution)/shard_map/pallas_call | solution.py:276
  (12 shorter events, 0.0 us)
Async XLA Ops:
  0.6 9.1 %copy-start.5 = (s32[256]{0:T(256)S(1)}, s32[256]{0:T(256)}, u32[]{:S(2)}) copy-start(s32[256]{0:T(256)} %owner_ref.5) | copy-start | bytes 3076
  0.6 13.0 %copy-start.1 = (f32[1,512,512]{2,1,0:T(8,128)S(1)}, f32[1,512,512]{2,1,0:T(8,128)}, u32[]{:S(2)}) copy-start(f32[1,512,512]{2,1,0:T(8,128)} %param.10) | copy-start | bytes 3145732
  0.7 13.0 %copy-start.2 = (f32[1,512,512]{2,1,0:T(8,128)S(1)}, f32[1,512,512]{2,1,0:T(8,128)}, u32[]{:S(2)}) copy-start(f32[1,512,512]{2,1,0:T(8,128)} %param.11) | copy-start | bytes 3145732
  0.7 13.0 %copy-start.7 = (s32[32]{0:T(128)S(1)}, s32[32]{0:T(128)}, u32[]{:S(2)}) copy-start(s32[32]{0:T(128)} %refresh_ref.1) | copy-start | bytes 388
  4.9 19.4 %collective-permute-start = (bf16[64,16,512]{2,1,0:T(8,128)(2,1)}, bf16[64,16,512]{2,1,0:T(8,128)(2,1)S(1)}, u32[]{:S(2)}, u32[]{:S(2)}) collective-permute-start(bf16[64,16,512]{2,1,0:T(8,128)(2,1)} %get-tuple-element.28), channel_id=1, source_target_pairs={{0,1},{1,0},{2,3},{3,2},{4,5},{5,4},{6,7},{7,6},{8,9},{9,8},{10,11... | collective-permute-start | bytes 3145736 | tf_op jit(solution)/shard_map/ppermute | solution.py:297
  5.0 19.1 %collective-permute-start.1 = (bf16[44,16,512]{2,1,0:T(8,128)(2,1)}, bf16[44,16,512]{2,1,0:T(8,128)(2,1)S(1)}, u32[]{:S(2)}, u32[]{:S(2)}) collective-permute-start(bf16[44,16,512]{2,1,0:T(8,128)(2,1)} %get-tuple-element.29), channel_id=1, source_target_pairs={{0,64},{1,193},{2,66},{3,195},{4,68},{5,197},{6,70},{7,199},{8,72}... | collective-permute-start | bytes 2162696 | tf_op jit(solution)/shard_map/ppermute | solution.py:297
  6.0 18.4 %collective-permute-start.2 = (bf16[44,16,512]{2,1,0:T(8,128)(2,1)}, bf16[44,16,512]{2,1,0:T(8,128)(2,1)S(1)}, u32[]{:S(2)}, u32[]{:S(2)}) collective-permute-start(bf16[44,16,512]{2,1,0:T(8,128)(2,1)} %get-tuple-element.30), channel_id=1, source_target_pairs={{0,193},{1,64},{2,195},{3,66},{4,197},{5,68},{6,199},{7,70},{8,201... | collective-permute-start | bytes 2162696 | tf_op jit(solution)/shard_map/ppermute | solution.py:297
  8.1 10.9 %collective-permute-start.3 = (bf16[20,16,512]{2,1,0:T(8,128)(2,1)}, bf16[20,16,512]{2,1,0:T(8,128)(2,1)S(1)}, u32[]{:S(2)}, u32[]{:S(2)}) collective-permute-start(bf16[20,16,512]{2,1,0:T(8,128)(2,1)} %get-tuple-element.33), channel_id=1, source_target_pairs={{0,32},{1,33},{2,34},{3,35},{4,36},{5,37},{6,38},{7,39},{8,40},{9,... | collective-permute-start | bytes 983048 | tf_op jit(solution)/shard_map/ppermute | solution.py:297
  9.7 13.6 %collective-permute-start.4 = (bf16[20,16,512]{2,1,0:T(8,128)(2,1)}, bf16[20,16,512]{2,1,0:T(8,128)(2,1)S(1)}, u32[]{:S(2)}, u32[]{:S(2)}) collective-permute-start(bf16[20,16,512]{2,1,0:T(8,128)(2,1)} %get-tuple-element.34), channel_id=1, source_target_pairs={{0,33},{1,32},{2,35},{3,34},{4,37},{5,36},{6,39},{7,38},{8,41},{9,... | collective-permute-start | bytes 983048 | tf_op jit(solution)/shard_map/ppermute | solution.py:297
  9.7 2.2 %copy-start = (bf16[1,256,16,512]{3,2,1,0:T(8,128)(2,1)S(1)}, bf16[1,256,16,512]{3,2,1,0:T(8,128)(2,1)}, u32[]{:S(2)}) copy-start(bf16[1,256,16,512]{3,2,1,0:T(8,128)(2,1)} %param.7) | copy-start | bytes 12582916
  11.9 0.7 copy-start.6
  12.6 1.2 %copy-start.3 = (f32[1,512,512]{2,1,0:T(8,128)S(1)}, f32[1,512,512]{2,1,0:T(8,128)}, u32[]{:S(2)}) copy-start(f32[1,512,512]{2,1,0:T(8,128)} %param.12) | copy-start | bytes 3145732
  12.6 1.5 %copy-start.4 = (f32[1,512,512]{2,1,0:T(8,128)S(1)}, f32[1,512,512]{2,1,0:T(8,128)}, u32[]{:S(2)}) copy-start(f32[1,512,512]{2,1,0:T(8,128)} %param.13) | copy-start | bytes 3145732
  24.6 11.5 %collective-permute-start.5 = (bf16[44,16,512]{2,1,0:T(8,128)(2,1)S(1)}, bf16[44,16,512]{2,1,0:T(8,128)(2,1)S(1)}, u32[]{:S(2)}, u32[]{:S(2)}) collective-permute-start(bf16[44,16,512]{2,1,0:T(8,128)(2,1)S(1)} %get-tuple-element.38.refs_6_), channel_id=1, source_target_pairs={{0,32},{1,65},{2,34},{3,67},{4,36},{5,69},{6,38},{7,71},{8,40},{9,... | collective-permute-start | bytes 2162696 | tf_op jit(solution)/shard_map/ppermute | solution.py:297
  26.3 9.8 %collective-permute-start.6 = (bf16[20,16,512]{2,1,0:T(8,128)(2,1)S(1)}, bf16[20,16,512]{2,1,0:T(8,128)(2,1)S(1)}, u32[]{:S(2)}, u32[]{:S(2)}) collective-permute-start(bf16[20,16,512]{2,1,0:T(8,128)(2,1)S(1)} %get-tuple-element.40), channel_id=1, source_target_pairs={{0,192},{1,193},{2,194},{3,195},{4,196},{5,197},{6,198},{7,199},{8... | collective-permute-start | bytes 983048 | tf_op jit(solution)/shard_map/ppermute | solution.py:297
  36.3 8.7 %collective-permute-start.7 = (bf16[22,16,512]{2,1,0:T(8,128)(2,1)S(1)}, bf16[22,16,512]{2,1,0:T(8,128)(2,1)S(1)}, u32[]{:S(2)}, u32[]{:S(2)}) collective-permute-start(bf16[22,16,512]{2,1,0:T(8,128)(2,1)S(1)} %get-tuple-element.42.refs_4_), channel_id=1, source_target_pairs={{0,192},{1,33},{2,194},{3,35},{4,196},{5,37},{6,198},{7,39},{8,200... | collective-permute-start | bytes 1081352 | tf_op jit(solution)/shard_map/ppermute | solution.py:297
  38.6 5.3 %collective-permute-start.8 = (bf16[10,16,512]{2,1,0:T(8,128)(2,1)S(1)}, bf16[10,16,512]{2,1,0:T(8,128)(2,1)S(1)}, u32[]{:S(2)}, u32[]{:S(2)}) collective-permute-start(bf16[10,16,512]{2,1,0:T(8,128)(2,1)S(1)} %get-tuple-element.44), channel_id=1, source_target_pairs={{0,64},{1,65},{2,66},{3,67},{4,68},{5,69},{6,70},{7,71},{8,72},{9,... | collective-permute-start | bytes 491528 | tf_op jit(solution)/shard_map/ppermute | solution.py:297

commit v5 on v4

--- a/solution.py
+++ b/solution.py
@@ -120,13 +120,13 @@
     core = lax.rem(slot_ref[0], 2)
     offset = 0
     for k, count in enumerate(counts):
-        same, other, own, out = refs[3 * k], refs[3 * k + 1], refs[3 * k + 2], refs[3 * n + 1 + k]
+        same, other, out = refs[2 * k], refs[2 * k + 1], refs[2 * n + 1 + k]
 
         @pl.loop(0, 2 * count, unroll=count)
-        def _(i, same=same, other=other, own=own, out=out, offset=offset, count=count):
+        def _(i, same=same, other=other, out=out, offset=offset, count=count):
             j = 2 * count * second + i
             f32 = jnp.float32
-            out[2 * i + core] = (same[j].astype(f32) + own[j].astype(f32)).astype(out.dtype)
+            out[2 * i + core] = same[j]
             out[2 * i + 1 - core] = (
                 other[j].astype(f32) + handed_ref[offset + j].astype(f32)
             ).astype(out.dtype)
@@ -324,8 +324,13 @@
         owner_of, refresh, slot, stats_and_roots, token
     )
     places = [count for _, count, _ in streams]
-    arrays = [x for three in zip(same, other, own) for x in three]
-    sent = first_sum(slot, places, 1, handed, arrays, token)
+    same = event(
+        [x for pair in zip(same, own) for x in pair],
+        [[(4 * n, [(2 * k, 0), (2 * k + 1, 0)])] for k, n in enumerate(places)],
+        (token,),
+    )
+    arrays = [x for pair in zip(same, other) for x in pair]
+    sent = first_sum(slot, places, 1, handed, arrays, same[0])
     got = steps(1, sent)
     kept = first_sum(slot, places, 0, handed, arrays, sent[0])
 

time: 75.2 us -> 75.1 us (level)
  transfers between devices with their start and end apart: 9 -> 9, of which waited for: 7 -> 5; matrix products, arithmetic and copies ran while one was open for 0% -> 0% of each run, Pallas kernels for 5% -> 5%
where the time goes in v5:
time: 75.1 us; the launch traced here: 74.9 us
  blocking collectives  27.4 us (36%)
  waiting for transfers between devices  23.1 us (31%)
  Pallas kernels  11.1 us (15%)
  starting transfers between devices  9.21 us (12%)
  local copies, waits for them, and re-layouts  3.33 us (4%)
  between operations  0.79 us (1%)
    all_to_all x1, blocking collectives, to_owners(): lax.all_to_all(x, 'owner', split_axis=0, concat_axis=0, tiled=True, axis_...  27.4 us
    ppermute x9, waiting for transfers between devices, send(): return lax.ppermute(x, AXES, route(n_slots, n_owner, *how))  23.1 us
    ppermute x9, starting transfers between devices, send(): return lax.ppermute(x, AXES, route(n_slots, n_owner, *how))  9.21 us
    pallas_call x2, Pallas kernels, pick(): pl.pallas_call(functools.partial(pick_kernel, plan, n_owner, chunks, len(...  5.31 us
    unnamed x16, local copies, waits for them, and re-layouts  3.33 us
    pallas_call x1, Pallas kernels, finish(): pl.pallas_call(finish_kernel, out_shape=out_shape, in_specs=[vmem] * 5, o...  2.55 us
    pallas_call x1, Pallas kernels, roots(): pl.pallas_call(roots_kernel, out_shape=[jax.ShapeDtypeStruct(stat.shape,...  2.33 us
  transfers between devices with their start and end apart: 9, of which 5 were waited for; matrix products, arithmetic and copies ran while one was open for 0% of the time, Pallas kernels for 5%

profile of v5, /device:TPU:6, one launch (start us, length us, event | category | flops | bytes accessed | tf_op | source)
XLA Modules:
  0.0 74.9 jit_solution(7218389221639567389)
XLA Ops:
  0.7 4.2 %shard_map.110 = (bf16[64,16,512]{2,1,0:T(8,128)(2,1)}, bf16[44,16,512]{2,1,0:T(8,128)(2,1)}, bf16[20,16,512]{2,1,0:T(8,128)(2,1)}, bf16[44,16,512]{2,1,0:T(8,12...) custom-call(s32[1]{0:T(128)} %bitcast.slot_ref, s32[256]{0:T(256)} %owner_ref.5, bf16[256,16,512]{2,1,0:T(8,128)(2,1)} %bitcast.13), custom_call_target="tpu_custom_call" | custom-call | bytes 1024 | tf_op jit(solution)/shard_map/pallas_call | solution.py:103
  4.9 0.1 collective-permute-start
  5.0 0.9 %collective-permute-start.1 = (bf16[44,16,512]{2,1,0:T(8,128)(2,1)}, bf16[44,16,512]{2,1,0:T(8,128)(2,1)S(1)}, u32[]{:S(2)}, u32[]{:S(2)}) collective-permute-start(bf16[44,16,512]{2,1,0:T(8,128)(2,1)} %get-tuple-element.31), channel_id=1, source_target_pairs={{0,64},{1,193},{2,66},{3,195},{4,68},{5,197},{6,70},{7,199},{8,72}... | collective-permute-start | bytes 2162696 | tf_op jit(solution)/shard_map/ppermute | solution.py:297
  6.0 2.1 %collective-permute-start.3 = (bf16[44,16,512]{2,1,0:T(8,128)(2,1)}, bf16[44,16,512]{2,1,0:T(8,128)(2,1)S(1)}, u32[]{:S(2)}, u32[]{:S(2)}) collective-permute-start(bf16[44,16,512]{2,1,0:T(8,128)(2,1)} %get-tuple-element.39), channel_id=1, source_target_pairs={{0,193},{1,64},{2,195},{3,66},{4,197},{5,68},{6,199},{7,70},{8,201... | collective-permute-start | bytes 2162696 | tf_op jit(solution)/shard_map/ppermute | solution.py:297
  8.1 1.6 %collective-permute-start.2 = (bf16[20,16,512]{2,1,0:T(8,128)(2,1)}, bf16[20,16,512]{2,1,0:T(8,128)(2,1)S(1)}, u32[]{:S(2)}, u32[]{:S(2)}) collective-permute-start(bf16[20,16,512]{2,1,0:T(8,128)(2,1)} %get-tuple-element.34), channel_id=1, source_target_pairs={{0,32},{1,33},{2,34},{3,35},{4,36},{5,37},{6,38},{7,39},{8,40},{9,... | collective-permute-start | bytes 983048 | tf_op jit(solution)/shard_map/ppermute | solution.py:297
  9.7 0.0 collective-permute-start.4
  9.7 2.2 %copy-done = bf16[1,256,16,512]{3,2,1,0:T(8,128)(2,1)S(1)} copy-done((bf16[1,256,16,512]{3,2,1,0:T(8,128)(2,1)S(1)}, bf16[1,256,16,512]{3,2,1,0:T(8,128)(2,1)}, u32[]{:S(2)}) %copy-start) | copy-done | bytes 4194328
  11.9 0.7 copy-done.6
  12.6 1.1 %shard_map.111 = (bf16[44,16,512]{2,1,0:T(8,128)(2,1)S(1)}, bf16[20,16,512]{2,1,0:T(8,128)(2,1)S(1)}, f32[8,128]{1,0:T(8,128)S(1)}) custom-call(s32[1]{0:T(128)} %bitcast.slot_ref, s32[256]{0:T(256)S(1)} %copy-done.5, bf16[256,16,512]{2,1,0:T(8,128)(2,1)S(1)} %bitcast.14, f32[8,128]{1,0:T(8,128)S(1)} %copy-done.6), custom_call_target="tpu_custom_call" | custom-call | bytes 1024 | tf_op jit(solution)/shard_map/pallas_call | solution.py:103
  13.7 0.1 copy-done.3
  13.8 0.3 copy-done.4
  14.1 2.3 %shard_map.112 = (f32[512,512]{1,0:T(8,128)}, f32[512,512]{1,0:T(8,128)}, f32[8,128]{1,0:T(8,128)S(1)}) custom-call(s32[256]{0:T(256)S(1)} %copy-done.5, s32[32]{0:T(128)S(1)} %copy-done.7, s32[1]{0:T(128)} %bitcast.slot_ref, f32[512,512]{1,0:T(8,128)S(1)} %bitcast.15, f32[512,512]{1,0:T(8,128)S(1)} %bitcast.17, f32[512,512]{1,0:T(8,128)S(1)} %bitcast.19, ...), custom_call_target="tpu_custom_call" | custom-call | bytes 1024 | tf_op jit(solution)/shard_map/pallas_call | solution.py:233
  16.4 2.5 %collective-permute-done.2.refs_2_ = bf16[20,16,512]{2,1,0:T(8,128)(2,1)S(1)} collective-permute-done((bf16[20,16,512]{2,1,0:T(8,128)(2,1)}, bf16[20,16,512]{2,1,0:T(8,128)(2,1)S(1)}, u32[]{:S(2)}, u32[]{:S(2)}) %collective-permute-start.2) | collective-permute-done | bytes 327712 | tf_op jit(solution)/shard_map/ppermute | solution.py:297
  19.0 5.1 %collective-permute-done.1.refs_0_ = bf16[44,16,512]{2,1,0:T(8,128)(2,1)S(1)} collective-permute-done((bf16[44,16,512]{2,1,0:T(8,128)(2,1)}, bf16[44,16,512]{2,1,0:T(8,128)(2,1)S(1)}, u32[]{:S(2)}, u32[]{:S(2)}) %collective-permute-start.1) | collective-permute-done | bytes 720928 | tf_op jit(solution)/shard_map/ppermute | solution.py:297
  24.1 0.3 shard_map.113
  24.4 0.0 collective-permute-done.4.refs_3_
  24.4 0.0 collective-permute-done.3.refs_1_
  24.4 0.0 collective-permute-done.handed_ref
  24.4 0.2 shard_map.114
  24.5 1.7 %collective-permute-start.5 = (bf16[44,16,512]{2,1,0:T(8,128)(2,1)S(1)}, bf16[44,16,512]{2,1,0:T(8,128)(2,1)S(1)}, u32[]{:S(2)}, u32[]{:S(2)}) collective-permute-start(bf16[44,16,512]{2,1,0:T(8,128)(2,1)S(1)} %get-tuple-element.42.refs_4_), channel_id=1, source_target_pairs={{0,32},{1,65},{2,34},{3,67},{4,36},{5,69},{6,38},{7,71},{8,40},{9,... | collective-permute-start | bytes 2162696 | tf_op jit(solution)/shard_map/ppermute | solution.py:297
  26.2 0.5 collective-permute-start.6
  26.7 0.1 shard_map.115
  26.9 9.1 %collective-permute-done.6.refs_2_ = bf16[20,16,512]{2,1,0:T(8,128)(2,1)S(1)} collective-permute-done((bf16[20,16,512]{2,1,0:T(8,128)(2,1)S(1)}, bf16[20,16,512]{2,1,0:T(8,128)(2,1)S(1)}, u32[]{:S(2)}, u32[]{:S(2)}) %collective-permute-start.6) | collective-permute-done | bytes 327712 | tf_op jit(solution)/shard_map/ppermute | solution.py:297
  36.0 0.0 collective-permute-done.5.refs_0_
  36.0 0.1 shard_map.116
  36.1 2.3 %collective-permute-start.7 = (bf16[22,16,512]{2,1,0:T(8,128)(2,1)S(1)}, bf16[22,16,512]{2,1,0:T(8,128)(2,1)S(1)}, u32[]{:S(2)}, u32[]{:S(2)}) collective-permute-start(bf16[22,16,512]{2,1,0:T(8,128)(2,1)S(1)} %get-tuple-element.46.refs_4_), channel_id=1, source_target_pairs={{0,192},{1,33},{2,194},{3,35},{4,196},{5,37},{6,198},{7,39},{8,200... | collective-permute-start | bytes 1081352 | tf_op jit(solution)/shard_map/ppermute | solution.py:297
  38.4 0.1 shard_map.117
  38.5 5.2 %collective-permute-done.8.refs_2_ = bf16[10,16,512]{2,1,0:T(8,128)(2,1)S(1)} collective-permute-done((bf16[10,16,512]{2,1,0:T(8,128)(2,1)S(1)}, bf16[10,16,512]{2,1,0:T(8,128)(2,1)S(1)}, u32[]{:S(2)}, u32[]{:S(2)}) %collective-permute-start.8) | collective-permute-done | bytes 163872 | tf_op jit(solution)/shard_map/ppermute | solution.py:297
  43.7 1.1 %collective-permute-done.7.refs_0_ = bf16[22,16,512]{2,1,0:T(8,128)(2,1)S(1)} collective-permute-done((bf16[22,16,512]{2,1,0:T(8,128)(2,1)S(1)}, bf16[22,16,512]{2,1,0:T(8,128)(2,1)S(1)}, u32[]{:S(2)}, u32[]{:S(2)}) %collective-permute-start.7) | collective-permute-done | bytes 360480 | tf_op jit(solution)/shard_map/ppermute | solution.py:297
  44.8 0.1 shard_map.118
  45.0 27.4 %all_to_all.5 = bf16[16,32,512]{2,1,0:T(8,128)(2,1)S(1)} all-to-all(bf16[16,32,512]{2,1,0:T(8,128)(2,1)S(1)} %bitcast.24), channel_id=1, replica_groups={{0,2,4,6,8,10,12,14,16,18,20,22,24,26,28,30},{1,3,5,7,9,11,13,15,17,19,..., dimensions={0} | all-to-all | bytes 1048576 | tf_op jit(solution)/shard_map/all_to_all | solution.py:310
  72.3 2.6 %shard_map.119 = (bf16[512,512]{1,0:T(8,128)(2,1)}, f32[512,512]{1,0:T(8,128)}, f32[512,512]{1,0:T(8,128)}) custom-call(bf16[512,512]{1,0:T(8,128)(2,1)S(1)} %bitcast.23, f32[512,512]{1,0:T(8,128)S(1)} %bitcast.16, f32[512,512]{1,0:T(8,128)S(1)} %bitcast.18, f32[512,512]{1,0:T(8,128)S(1)} %bitcast.20, f32[512,512]{1,0:T(8,128)S(1)} %bitcast.22), custom_call_target="tpu_custom_call" | custom-call | flops 1073741824 | bytes 7340032 | tf_op jit(solution)/shard_map/pallas_call | solution.py:276
  (13 shorter events, 0.0 us)
Async XLA Ops:
  0.6 9.0 %copy-start.5 = (s32[256]{0:T(256)S(1)}, s32[256]{0:T(256)}, u32[]{:S(2)}) copy-start(s32[256]{0:T(256)} %owner_ref.5) | copy-start | bytes 3076
  0.6 13.0 %copy-start.1 = (f32[1,512,512]{2,1,0:T(8,128)S(1)}, f32[1,512,512]{2,1,0:T(8,128)}, u32[]{:S(2)}) copy-start(f32[1,512,512]{2,1,0:T(8,128)} %param.10) | copy-start | bytes 3145732
  0.7 13.0 %copy-start.2 = (f32[1,512,512]{2,1,0:T(8,128)S(1)}, f32[1,512,512]{2,1,0:T(8,128)}, u32[]{:S(2)}) copy-start(f32[1,512,512]{2,1,0:T(8,128)} %param.11) | copy-start | bytes 3145732
  0.7 13.0 %copy-start.7 = (s32[32]{0:T(128)S(1)}, s32[32]{0:T(128)}, u32[]{:S(2)}) copy-start(s32[32]{0:T(128)} %refresh_ref.1) | copy-start | bytes 388
  4.9 19.4 %collective-permute-start = (bf16[64,16,512]{2,1,0:T(8,128)(2,1)}, bf16[64,16,512]{2,1,0:T(8,128)(2,1)S(1)}, u32[]{:S(2)}, u32[]{:S(2)}) collective-permute-start(bf16[64,16,512]{2,1,0:T(8,128)(2,1)} %get-tuple-element.30), channel_id=1, source_target_pairs={{0,1},{1,0},{2,3},{3,2},{4,5},{5,4},{6,7},{7,6},{8,9},{9,8},{10,11... | collective-permute-start | bytes 3145736 | tf_op jit(solution)/shard_map/ppermute | solution.py:297
  5.0 19.1 %collective-permute-start.1 = (bf16[44,16,512]{2,1,0:T(8,128)(2,1)}, bf16[44,16,512]{2,1,0:T(8,128)(2,1)S(1)}, u32[]{:S(2)}, u32[]{:S(2)}) collective-permute-start(bf16[44,16,512]{2,1,0:T(8,128)(2,1)} %get-tuple-element.31), channel_id=1, source_target_pairs={{0,64},{1,193},{2,66},{3,195},{4,68},{5,197},{6,70},{7,199},{8,72}... | collective-permute-start | bytes 2162696 | tf_op jit(solution)/shard_map/ppermute | solution.py:297
  6.0 18.4 %collective-permute-start.3 = (bf16[44,16,512]{2,1,0:T(8,128)(2,1)}, bf16[44,16,512]{2,1,0:T(8,128)(2,1)S(1)}, u32[]{:S(2)}, u32[]{:S(2)}) collective-permute-start(bf16[44,16,512]{2,1,0:T(8,128)(2,1)} %get-tuple-element.39), channel_id=1, source_target_pairs={{0,193},{1,64},{2,195},{3,66},{4,197},{5,68},{6,199},{7,70},{8,201... | collective-permute-start | bytes 2162696 | tf_op jit(solution)/shard_map/ppermute | solution.py:297
  8.1 10.9 %collective-permute-start.2 = (bf16[20,16,512]{2,1,0:T(8,128)(2,1)}, bf16[20,16,512]{2,1,0:T(8,128)(2,1)S(1)}, u32[]{:S(2)}, u32[]{:S(2)}) collective-permute-start(bf16[20,16,512]{2,1,0:T(8,128)(2,1)} %get-tuple-element.34), channel_id=1, source_target_pairs={{0,32},{1,33},{2,34},{3,35},{4,36},{5,37},{6,38},{7,39},{8,40},{9,... | collective-permute-start | bytes 983048 | tf_op jit(solution)/shard_map/ppermute | solution.py:297
  9.7 14.7 %collective-permute-start.4 = (bf16[20,16,512]{2,1,0:T(8,128)(2,1)}, bf16[20,16,512]{2,1,0:T(8,128)(2,1)S(1)}, u32[]{:S(2)}, u32[]{:S(2)}) collective-permute-start(bf16[20,16,512]{2,1,0:T(8,128)(2,1)} %get-tuple-element.41), channel_id=1, source_target_pairs={{0,33},{1,32},{2,35},{3,34},{4,37},{5,36},{6,39},{7,38},{8,41},{9,... | collective-permute-start | bytes 983048 | tf_op jit(solution)/shard_map/ppermute | solution.py:297
  9.7 2.2 %copy-start = (bf16[1,256,16,512]{3,2,1,0:T(8,128)(2,1)S(1)}, bf16[1,256,16,512]{3,2,1,0:T(8,128)(2,1)}, u32[]{:S(2)}) copy-start(bf16[1,256,16,512]{3,2,1,0:T(8,128)(2,1)} %param.7) | copy-start | bytes 12582916
  11.9 0.7 copy-start.6
  12.6 1.2 %copy-start.3 = (f32[1,512,512]{2,1,0:T(8,128)S(1)}, f32[1,512,512]{2,1,0:T(8,128)}, u32[]{:S(2)}) copy-start(f32[1,512,512]{2,1,0:T(8,128)} %param.12) | copy-start | bytes 3145732
  12.6 1.5 %copy-start.4 = (f32[1,512,512]{2,1,0:T(8,128)S(1)}, f32[1,512,512]{2,1,0:T(8,128)}, u32[]{:S(2)}) copy-start(f32[1,512,512]{2,1,0:T(8,128)} %param.13) | copy-start | bytes 3145732
  24.5 11.4 %collective-permute-start.5 = (bf16[44,16,512]{2,1,0:T(8,128)(2,1)S(1)}, bf16[44,16,512]{2,1,0:T(8,128)(2,1)S(1)}, u32[]{:S(2)}, u32[]{:S(2)}) collective-permute-start(bf16[44,16,512]{2,1,0:T(8,128)(2,1)S(1)} %get-tuple-element.42.refs_4_), channel_id=1, source_target_pairs={{0,32},{1,65},{2,34},{3,67},{4,36},{5,69},{6,38},{7,71},{8,40},{9,... | collective-permute-start | bytes 2162696 | tf_op jit(solution)/shard_map/ppermute | solution.py:297
  26.2 9.8 %collective-permute-start.6 = (bf16[20,16,512]{2,1,0:T(8,128)(2,1)S(1)}, bf16[20,16,512]{2,1,0:T(8,128)(2,1)S(1)}, u32[]{:S(2)}, u32[]{:S(2)}) collective-permute-start(bf16[20,16,512]{2,1,0:T(8,128)(2,1)S(1)} %get-tuple-element.44), channel_id=1, source_target_pairs={{0,192},{1,193},{2,194},{3,195},{4,196},{5,197},{6,198},{7,199},{8... | collective-permute-start | bytes 983048 | tf_op jit(solution)/shard_map/ppermute | solution.py:297
  36.1 8.7 %collective-permute-start.7 = (bf16[22,16,512]{2,1,0:T(8,128)(2,1)S(1)}, bf16[22,16,512]{2,1,0:T(8,128)(2,1)S(1)}, u32[]{:S(2)}, u32[]{:S(2)}) collective-permute-start(bf16[22,16,512]{2,1,0:T(8,128)(2,1)S(1)} %get-tuple-element.46.refs_4_), channel_id=1, source_target_pairs={{0,192},{1,33},{2,194},{3,35},{4,196},{5,37},{6,198},{7,39},{8,200... | collective-permute-start | bytes 1081352 | tf_op jit(solution)/shard_map/ppermute | solution.py:297
  38.4 5.3 %collective-permute-start.8 = (bf16[10,16,512]{2,1,0:T(8,128)(2,1)S(1)}, bf16[10,16,512]{2,1,0:T(8,128)(2,1)S(1)}, u32[]{:S(2)}, u32[]{:S(2)}) collective-permute-start(bf16[10,16,512]{2,1,0:T(8,128)(2,1)S(1)} %get-tuple-element.48), channel_id=1, source_target_pairs={{0,64},{1,65},{2,66},{3,67},{4,68},{5,69},{6,70},{7,71},{8,72},{9,... | collective-permute-start | bytes 491528 | tf_op jit(solution)/shard_map/ppermute | solution.py:297
